TPU v7x, 128 devices: a whole 4x4x4 slice. The times are simulated.
128 devices in a mesh: group: 2 (over core), fsdp: 8 (over z, x_hi), tensor: 8 (over x_lo, y).
Axes of the slice: x: 4 (x_hi: 2, x_lo: 2; x = x_hi * 2 + x_lo), y: 4, z: 4, core: 2. Of those that a mesh axis runs over, the one named last changes fastest.
Arguments:
- master: float32 [8192, 6144], P('tensor', ('group', 'fsdp')), may hold values from -6 to 6
- moment: float32 [8192, 6144], P('tensor', ('group', 'fsdp')), may hold values from -4 to 4
- second: float32 [8192, 6144], P('tensor', ('group', 'fsdp')), may hold values from 0.001 to 0.2
- gradient: bfloat16 [8192, 6144], P('tensor', ('group', 'fsdp')), may hold values from -20000 to 20000
- prior_weights: bfloat16 [8192, 6144], P(None, 'tensor'), may hold values from -6 to 6
- tokens: bfloat16 [16, 1024, 8192], P(('group', 'fsdp'), None, 'tensor'), may hold values from -5000 to 5000
- norm_gain: float32 [8192], replicated, may hold values from 0.6 to 24
- segment_ids: int32 [16, 1024], P(('group', 'fsdp')), may hold values from 0 to 3, never falling along the last dimension, each value on 1 to 512 neighbouring positions
Outputs:
- new_master: float32 [8192, 6144], P('tensor', ('group', 'fsdp'))
- new_moment: float32 [8192, 6144], P('tensor', ('group', 'fsdp'))
- new_second: float32 [8192, 6144], P('tensor', ('group', 'fsdp'))
- attended: bfloat16 [16, 1024, 4096], P(('group', 'fsdp'), None, 'tensor')
Inputs may be any that keep to these rules, and one draw needn't show every extreme that they name: `segment_ids`: ids never fall along a row; a document holds at most half of a row's tokens.
All inputs are finite; a program needn't handle non-finite values.
Results may differ from a plain program's by a relative error of at most 0.04.
The roundings to bfloat16 on the way count: a program that leaves them out, or rounds other values in their place, can miss the bound.
Values may be sent and summed in bfloat16 or wider, within the bound.
A program may use at most 192 MiB of HBM per device.

v0:
```python
import math

import jax
import jax.numpy as jnp
from jax import lax
from jax.sharding import PartitionSpec as P

D = 8192
HD = 128
QPK = 4
QKV = 6144


learn_rate = 0.01
decay_rate = 0.1
clip_rms = 0.25
first_fix = 1.0 - math.exp(200.0 * math.log(0.9))
second_fix = 1.0 - math.exp(200.0 * math.log(0.95))
mix_share = 0.6


def spread(block, axis, source):
    block = jnp.where(lax.axis_index(axis) == source, block, jnp.zeros_like(block))
    return lax.psum(block, axis)


def rotary(values, token_count):
    head_width = values.shape[-1]
    half_width = head_width // 2
    places = jnp.arange(token_count).astype(jnp.float32)
    frequencies = 500000.0 ** (-(jnp.arange(half_width).astype(jnp.float32) * 2.0 / head_width))
    angles = places[:, None] * frequencies[None, :]
    cosine = jnp.cos(angles)[:, None, :]
    sine_table = jnp.sin(angles)[:, None, :]
    front_half = values[..., :half_width]
    back_half = values[..., half_width:]
    return jnp.concatenate(
        [
            front_half * cosine - back_half * sine_table,
            back_half * cosine + front_half * sine_table,
        ],
        axis=-1,
    )


def attend(projected, segments):
    token_count = projected.shape[0]
    groups = projected.shape[1]
    queries = rotary(projected[:, :, :QPK, :].reshape(token_count, groups * QPK, HD), token_count)
    queries = queries.astype(jnp.bfloat16).reshape(token_count, groups, QPK, HD)
    keys = rotary(projected[:, :, QPK, :], token_count).astype(jnp.bfloat16)
    values = projected[:, :, QPK + 1, :].astype(jnp.bfloat16)
    scores = jnp.einsum(
        "qgph,kgh->gpqk", queries, keys, preferred_element_type=jnp.float32
    ) * HD ** (-0.5)
    places = jnp.arange(token_count)
    allowed = (segments[:, None] == segments[None, :]) & (places[:, None] >= places[None, :])
    scores = jnp.where(allowed[None, None], scores, -jnp.inf)
    row_top = jnp.max(scores, axis=-1, keepdims=True)
    weights = jnp.exp(scores - row_top)
    weights_half = (weights / jnp.sum(weights, axis=-1, keepdims=True)).astype(jnp.bfloat16)
    output = jnp.einsum("gpqk,kgh->qgph", weights_half, values, preferred_element_type=jnp.float32)
    return output.reshape(token_count, groups * QPK * HD).astype(jnp.bfloat16)


def shards(master, moment, second, gradient, prior_weights, tokens, norm_gain, segment_ids):
    grad_values = gradient.astype(jnp.float32)
    local_sq = jnp.sum(grad_values * grad_values)
    overall = lax.psum(local_sq, ("group", "fsdp", "tensor"))
    clip_factor = jnp.minimum(1.0, clip_rms * math.sqrt(D * QKV) / (jnp.sqrt(overall) + 1e-06))
    clipped = clip_factor * grad_values
    new_moment = 0.9 * moment + 0.1 * clipped
    new_second = 0.95 * second + 0.05 * clipped * clipped
    update = (
        new_moment / first_fix / (jnp.sqrt(new_second / second_fix) + 1e-08) + decay_rate * master
    )
    new_master = master - learn_rate * update
    policy_half = new_master.astype(jnp.bfloat16)
    token_count = tokens.shape[1]
    feature_share = tokens.shape[2]
    values = tokens[0].astype(jnp.float32)
    part_sq = jnp.sum(values * values, axis=1)
    row_sq = lax.psum(part_sq, "tensor")
    inverse = lax.rsqrt(row_sq / D + 1e-05)
    gain_part = lax.dynamic_slice_in_dim(
        norm_gain, lax.axis_index("tensor") * feature_share, feature_share
    )
    normed_part = (values * inverse[:, None] * gain_part[None, :]).astype(jnp.bfloat16)
    normed = lax.all_gather(normed_part, "tensor", axis=1, tiled=True)
    group_count = lax.axis_size(("group", "fsdp"))
    tensor_count = lax.axis_size("tensor")
    panel_width = prior_weights.shape[1]
    column_rows = lax.all_gather(policy_half, "tensor", axis=0, tiled=True)
    tensor_index = lax.axis_index("tensor")
    blocks_per_panel = group_count // tensor_count
    received = []
    for offset in range(blocks_per_panel):
        received.append(
            spread(column_rows, ("group", "fsdp"), tensor_index * blocks_per_panel + offset)
        )
    panel = jnp.concatenate(received, axis=1)
    mixed_panel = (
        mix_share * panel.astype(jnp.float32)
        + (1.0 - mix_share) * prior_weights.astype(jnp.float32)
    ).astype(jnp.bfloat16)
    projected = jnp.dot(normed, mixed_panel, preferred_element_type=jnp.float32) * D ** (-0.5)
    local_groups = panel_width // ((QPK + 2) * HD)
    attended = attend(projected.reshape(token_count, local_groups, QPK + 2, HD), segment_ids[0])
    return (new_master, new_moment, new_second, attended[None])


def solution(mesh):
    in_specs = (
        P("tensor", ("group", "fsdp")),
        P("tensor", ("group", "fsdp")),
        P("tensor", ("group", "fsdp")),
        P("tensor", ("group", "fsdp")),
        P(None, "tensor"),
        P(("group", "fsdp"), None, "tensor"),
        P(),
        P(("group", "fsdp"), None),
    )
    out_specs = (
        P("tensor", ("group", "fsdp")),
        P("tensor", ("group", "fsdp")),
        P("tensor", ("group", "fsdp")),
        P(("group", "fsdp"), None, "tensor"),
    )
    return jax.shard_map(shards, mesh=mesh, in_specs=in_specs, out_specs=out_specs, check_vma=False)
```

profile of v0, /device:TPU:1, one launch (start us, length us, event | category | flops | bytes accessed | tf_op | source)
XLA Modules:
  0.0 918.7 jit_solution(3932784304095003087)
XLA Ops:
  7.2 0.0 all-gather.5.cloned.1.call-start
  7.2 2.1 fusion.17
  9.4 68.7 %psum.28 = f32[]{:T(128)} all-reduce(f32[]{:T(128)} %fusion.17), channel_id=1, replica_groups=mesh['group'=2,'fsdp'=8,'tensor'=8] {'group','fsdp','tensor'}, use_global_device_ids=true, to_apply=%region_1.0 | all-reduce | flops 1 | bytes 8 | tf_op jit(solution)/shard_map/psum | solution.py:69
  78.8 5.8 fusion.46
  84.6 0.0 all-gather.5.cloned.1.call-update
  84.6 0.0 all-reduce.3.cloned.1.call-start
  84.7 68.8 %all-gather.5.cloned.1.call-done = bf16[8192,384]{1,0:T(8,128)(2,1)} async-done(((bf16[1024,384]{1,0:T(8,128)(2,1)}), bf16[8192,384]{1,0:T(8,128)(2,1)}) %all-gather.5.cloned.1.call-update) | async-done | bytes 6291472 | tf_op jit(solution)/shard_map/all_gather | solution.py:93
  153.4 8.3 broadcast_select_fusion.1
  161.8 0.0 all-reduce.3.cloned.1.call-update
  161.8 0.0 all-gather.3.cloned.1.call-start
  161.8 0.8 dynamic_slice.3
  162.7 0.7 copy-done
  163.4 0.5 fusion.10
  163.9 13.5 %psum.29 = f32[1024]{0:T(1024)S(1)} all-reduce(f32[1024]{0:T(1024)S(1)} %fusion.10), channel_id=1, replica_groups=mesh['group'=2,'fsdp'=8,'tensor'=8] {'tensor'}, use_global_device_ids=true, to_apply=%region_3.0 | all-reduce | flops 1024 | bytes 8192 | tf_op jit(solution)/shard_map/psum | solution.py:83
  177.4 1.9 fusion.12
  179.3 0.0 all-gather.3.cloned.1.call-update
  179.3 3.2 multiply_cosine_fusion
  182.5 1.6 fusion.13
  184.1 511.2 %all-reduce.3.cloned.1.call-done = (bf16[8192,384]{1,0:T(8,128)(2,1)}, bf16[8192,384]{1,0:T(8,128)(2,1)}) async-done(((bf16[8192,384]{1,0:T(8,128)(2,1)}, bf16[8192,384]{1,0:T(8,128)(2,1)}), (bf16[8192,384]{1,0:T(8,128)(2,1)}, bf16[8192,384]{1,0:T(8,128)(2,1)})) %all-reduce.3.cloned.1.call-update) | async-done | bytes 12582928 | tf_op jit(solution)/shard_map/psum | solution.py:24
  695.3 171.9 %all-gather.3.cloned.1.call-done = bf16[1024,8192]{1,0:T(8,128)(2,1)} async-done(((bf16[1024,1024]{1,0:T(8,128)(2,1)}), bf16[1024,8192]{1,0:T(8,128)(2,1)}) %all-gather.3.cloned.1.call-update) | async-done | bytes 16777232 | tf_op jit(solution)/shard_map/all_gather | solution.py:89
  867.2 19.0 %fusion.14 = f32[1024,768]{0,1:T(8,128)S(1)} fusion(bf16[1024,8192]{1,0:T(8,128)(2,1)} %all-gather.3.cloned.1.call-done, bf16[8192,768]{1,0:T(8,128)(2,1)} %param.12, bf16[8192,384]{1,0:T(8,128)(2,1)} %get-tuple-element.8, bf16[8192,384]{1,0:T(8,128)(2,1)} %get-tuple-element.9), kind=kOutput, calls=%fused_computation.28 | convolution fusion | flops 12942311424 | bytes 45088768 | tf_op jit(solution)/shard_map/dot_general | solution.py:106
  886.3 1.6 slice.33
  887.9 0.7 copy-done.2
  888.6 0.8 slice.30
  889.4 1.9 copy.18
  891.3 1.2 copy.17
  892.6 2.4 fusion.39
  895.0 1.8 subtract_convert_fusion
  896.8 3.8 fusion.1
  900.6 3.7 fusion
  904.3 6.5 fusion.19
  910.8 1.3 copy.15
  (9 shorter events, 0.0 us)
Async XLA Ops:
  7.2 146.3 %all-gather.5.cloned.1.call-start = ((), (), s32[]{:S(2)}) async-start(), calls=%async_computation.1 | async-start | bytes 7077888 | tf_op jit(solution)/shard_map/all_gather | solution.py:93
  84.6 610.7 %all-reduce.3.cloned.1.call-start = ((), (), s32[]{:S(2)}) async-start(), calls=%async_computation.2 | async-start | bytes 25165824 | tf_op jit(solution)/shard_map/psum | solution.py:24
  161.8 1.6 copy-start
  161.8 705.4 %all-gather.3.cloned.1.call-start = ((), (), s32[]{:S(2)}) async-start(), calls=%async_computation | async-start | bytes 18874368 | tf_op jit(solution)/shard_map/all_gather | solution.py:89
  163.8 18.7 %copy-start.3 = (s32[1,1024]{1,0:T(1,128)S(1)}, s32[1,1024]{1,0:T(1,128)}, u32[]{:S(2)}) copy-start(s32[1,1024]{1,0:T(1,128)} %param.15) | copy-start | bytes 12292
  886.3 2.3 copy-start.2
  892.6 4.2 copy-start.1
Sparse Core Ops, SparseCore 0:
  84.7 68.6 all-gather.4
  161.9 533.3 all-reduce.2
  697.0 170.1 all-gather.2
where the time goes:
time: 919 us
  waiting for transfers between devices  752 us (82%)
  blocking collectives  82.2 us (9%)
  other arithmetic  31.3 us (3%)
  matrix products  29.4 us (3%)
  between operations  14.6 us (2%)
    psum x1, waiting for transfers between devices, spread(): return lax.psum(block, axis)  511 us
    all_gather x1, waiting for transfers between devices, shards(): normed = lax.all_gather(normed_part, 'tensor', axis=1, tiled=True)  172 us
    all_gather x1, waiting for transfers between devices, shards(): column_rows = lax.all_gather(policy_half, 'tensor', axis=0, tiled=True)  68.8 us
    psum x1, blocking collectives, shards(): overall = lax.psum(local_sq, ('group', 'fsdp', 'tensor'))  68.7 us
    dot_general x1, matrix products, shards(): jnp.dot(normed, mixed_panel, preferred_element_type=jnp.float32)  19 us
  transfers between devices with their start and end apart: 3, of which 3 were waited for; matrix products, arithmetic and copies ran while one was open for 1% of the time, Pallas kernels for 0%

commit v1 on v0

v1 whole, which is shorter than its diff:
```python
import functools
import math

import jax
import jax.numpy as jnp
import numpy as np
from jax import lax
from jax.experimental import pallas as pl
from jax.experimental.pallas import tpu as pltpu
from jax.sharding import PartitionSpec as P

D = 8192
HD = 128
QPK = 4
QKV = 6144

learn_rate = 0.01
decay_rate = 0.1
clip_rms = 0.25
first_fix = 1.0 - math.exp(200.0 * math.log(0.9))
second_fix = 1.0 - math.exp(200.0 * math.log(0.95))
mix_share = 0.6

MESH = pl.DeviceIdType.MESH
F32 = jnp.float32
BF16 = jnp.bfloat16
SUM_TYPE = BF16
TOK = 1024
FEAT = 1024
COLS = 384
PIECES = 4
PIECE = TOK // PIECES
ORDER = (2, 1, 0)


def rotary_tables():
    places = np.arange(TOK).astype(np.float32)
    lanes = np.arange(HD // 2).astype(np.float32)
    frequencies = np.power(500000.0, -(lanes * np.float32(2.0) / np.float32(HD)).astype(np.float64))
    angles = places[:, None] * frequencies.astype(np.float32)[None, :]
    cosine = np.cos(angles.astype(np.float64)).astype(np.float32)
    sine = np.sin(angles.astype(np.float64)).astype(np.float32)
    return np.stack(
        [np.concatenate([cosine, cosine], 1), np.concatenate([-sine, sine], 1)]
    ).astype(np.float32)


def adam(master, moment, second, grad, clip):
    clipped = clip * grad
    new_moment = 0.9 * moment + 0.1 * clipped
    new_second = 0.95 * second + 0.05 * clipped * clipped
    update = (
        new_moment / first_fix / (jnp.sqrt(new_second / second_fix) + 1e-08) + decay_rate * master
    )
    return master - learn_rate * update, new_moment, new_second


def push(src, dst, send, recv, where):
    return pltpu.make_async_remote_copy(
        src_ref=src, dst_ref=dst, send_sem=send, recv_sem=recv, device_id=where, device_id_type=MESH
    )


def project_kernel(
    master_ref, moment_ref, second_ref, grad_ref, prior_ref, tok_ref, gain_ref, table_ref,
    qkv_ref, clip_ref,
    raw, normed, w, mas, mom, sec, gra, inv, msg_a, msg_b, s1_out, s1_in, pri, own, ps_out, ps_in,
    load_sem, tok_s, tok_r, fwd_s, fwd_r, a_s, a_r, b_s, b_r, pri_s, pri_r, s1_s, s1_r, hx_s, hx_r,
    z_s, z_r, zf_s, zf_r, sib_s, sib_r, ps_s, ps_r,
):
    g = lax.axis_index("group")
    f = lax.axis_index("fsdp")
    t = lax.axis_index("tensor")
    z, h = f // 2, f % 2
    l, y = t // 4, t % 4
    y_up, y_down, y_far = (y + 1) % 4, (y + 3) % 4, (y + 2) % 4
    z_up, z_down, z_far = (z + 1) % 4, (z + 3) % 4, (z + 2) % 4
    at_y_up, at_y_down = (g, f, l * 4 + y_up), (g, f, l * 4 + y_down)
    at_z_up, at_z_down = (g, z_up * 2 + h, t), (g, z_down * 2 + h, t)
    at_x = (g, f, (1 - l) * 4 + y)
    at_h = (g, z * 2 + (1 - h), t)
    at_core = (1 - g, f, t)
    at_swap = (g, y * 2 + h, l * 4 + z)
    straight = y == z
    mine = g * 8 + f

    loads = [
        pltpu.make_async_copy(grad_ref, gra, load_sem.at[0]),
        pltpu.make_async_copy(tok_ref, raw.at[y], load_sem.at[1]),
        pltpu.make_async_copy(master_ref, mas, load_sem.at[2]),
        pltpu.make_async_copy(moment_ref, mom, load_sem.at[3]),
        pltpu.make_async_copy(second_ref, sec, load_sem.at[4]),
    ]
    for load in loads:
        load.start()
    prior_cols = pl.ds(pl.multiple_of(h * COLS, 128), COLS)
    prior_here = pltpu.make_async_copy(
        prior_ref.at[pl.ds(pl.multiple_of((l * 4 + z) * FEAT, FEAT), FEAT), prior_cols], pri, load_sem.at[5]
    )
    prior_push = push(
        prior_ref.at[pl.ds(pl.multiple_of(((1 - l) * 4 + z) * FEAT, FEAT), FEAT), prior_cols],
        pri, pri_s, pri_r, at_x,
    )
    holds_prior = g == l

    peers_a = [(g, f, (t + d) % 8) for d in range(1, 8)]
    places_b = [(mine + d) % 16 for d in range(1, 16)]
    peers_b = [(place // 8, place % 8, t) for place in places_b]

    barrier = pltpu.get_barrier_semaphore()
    for peer in peers_a + peers_b:
        pl.semaphore_signal(barrier, inc=1, device_id=peer, device_id_type=MESH)

    @pl.when(jnp.logical_not(straight))
    def _():
        pl.semaphore_signal(barrier, inc=1, device_id=at_swap, device_id_type=MESH)
        pl.semaphore_wait(barrier, 23)

    @pl.when(straight)
    def _():
        pl.semaphore_wait(barrier, 22)

    tok_pushes = []
    for p in range(PIECES):
        rows = pl.ds(p * PIECE, PIECE)
        for way, where in ((0, at_y_up), (1, at_y_down)):
            copy = push(tok_ref.at[rows, :], raw.at[y, rows, :], tok_s.at[way, p], tok_r.at[way, p], where)
            copy.start()
            tok_pushes.append(copy)

    @pl.when(holds_prior)
    def _():
        prior_push.start()
        prior_here.start()

    loads[0].wait()

    def grad_sum(i, total):
        v = gra[pl.ds(pl.multiple_of(i * 64, 64), 64), :].astype(F32)
        return total + jnp.sum((v * v).reshape(8, 8, COLS), axis=0)

    total = lax.fori_loop(0, FEAT // 64, grad_sum, jnp.zeros((8, COLS), F32))
    msg_a[t, 8:16, :] = total[:, 0:128] + total[:, 128:256] + total[:, 256:384]
    loads[1].wait()
    for i in range(8):
        part = jnp.zeros((128, 128), F32)
        for j in range(FEAT // 128):
            v = raw[y, i * 128:(i + 1) * 128, j * 128:(j + 1) * 128].astype(F32)
            part = part + v * v
        msg_a[t, i:i + 1, :] = jnp.sum(part.T, axis=0, keepdims=True)
    a_pushes = [
        push(msg_a.at[t], msg_a.at[t], a_s.at[d], a_r.at[d], peer) for d, peer in enumerate(peers_a)
    ]
    for copy in a_pushes:
        copy.start()
    for d in range(7):
        source = (t + 7 - d) % 8
        push(msg_a.at[source], msg_a.at[source], a_s.at[d], a_r.at[d], peers_a[d]).wait_recv()
    sums = msg_a[0]
    for s in range(1, 8):
        sums = sums + msg_a[s]
    msg_b[mine] = sums[8:16, :]
    b_pushes = [
        push(msg_b.at[mine], msg_b.at[mine], b_s.at[d], b_r.at[d], peer) for d, peer in enumerate(peers_b)
    ]
    for copy in b_pushes:
        copy.start()
    inverse = lax.rsqrt(sums[0:8, :] / D + 1e-05)
    for i in range(8):
        inv[i * 128:(i + 1) * 128, :] = jnp.broadcast_to(inverse[i:i + 1, :], (128, 128)).T
    for d in range(15):
        source = (mine + 15 - d) % 16
        push(msg_b.at[source], msg_b.at[source], b_s.at[d], b_r.at[d], peers_b[d]).wait_recv()
    sums = msg_b[0]
    for s in range(1, 16):
        sums = sums + msg_b[s]
    overall = jnp.broadcast_to(jnp.sum(sums, keepdims=True), (8, 128))
    clip_ref[...] = jnp.minimum(1.0, clip_rms * math.sqrt(D * QKV) / (jnp.sqrt(overall) + 1e-06))

    for load in loads[2:]:
        load.wait()
    s1_pushes, s1_copies = [None] * 3, [None] * 3
    for c in ORDER:
        cols = slice(c * 128, (c + 1) * 128)

        def step(i, carry, c=c, cols=cols):
            rows = pl.ds(pl.multiple_of(i * 64, 64), 64)
            updated, _, _ = adam(
                mas[rows, cols], mom[rows, cols], sec[rows, cols], gra[rows, cols].astype(F32), clip_ref[0:1, :]
            )
            s1_out[c, rows, :] = updated.astype(BF16)
            return carry

        lax.fori_loop(0, FEAT // 64, step, 0)
        s1_pushes[c] = push(s1_out.at[c], s1_in.at[c], s1_s.at[c], s1_r.at[c], at_swap)
        s1_copies[c] = pltpu.make_async_copy(s1_out.at[c], s1_in.at[c], s1_r.at[c])

        @pl.when(jnp.logical_not(straight))
        def _(c=c):
            s1_pushes[c].start()

        @pl.when(straight)
        def _(c=c):
            s1_copies[c].start()

    def normalize(block):
        gain = gain_ref[l * 4 + block]

        def step(i, carry):
            rows = pl.ds(pl.multiple_of(i * 64, 64), 64)
            scale = jnp.concatenate([inv[rows, :]] * (FEAT // 128), axis=1)
            normed[block, rows, :] = (raw[block, rows, :].astype(F32) * scale * gain).astype(BF16)
            return carry

        lax.fori_loop(0, TOK // 64, step, 0)

    normalize(y)

    @pl.when(holds_prior)
    def _():
        prior_here.wait()

    @pl.when(jnp.logical_not(holds_prior))
    def _():
        prior_push.wait_recv()

    here = pl.ds(pl.multiple_of(h * 128, 128), 128)
    hx_pushes = [None] * 3
    for c in ORDER:
        @pl.when(jnp.logical_not(straight))
        def _(c=c):
            s1_pushes[c].wait_recv()

        @pl.when(straight)
        def _(c=c):
            s1_copies[c].wait()

        def step(i, carry, c=c):
            rows = pl.ds(pl.multiple_of(i * 64, 64), 64)
            policy = s1_in[c, rows, :].astype(F32)
            prior = pri[rows, c * 128:(c + 1) * 128].astype(F32)
            w[c, z, g, rows, here] = (mix_share * policy + (1.0 - mix_share) * prior).astype(BF16)
            return carry

        lax.fori_loop(0, FEAT // 64, step, 0)
        block = w.at[c, z, g, :, here]
        hx_pushes[c] = push(block, block, hx_s.at[c], hx_r.at[c], at_h)
        hx_pushes[c].start()

    z_pushes, zf_pushes, sib_pushes = {}, {}, {}

    def share(c, slot, where):
        block = w.at[c, where, g]
        sib_pushes[c, slot] = push(block, block, sib_s.at[c, slot], sib_r.at[c, slot], at_core)
        sib_pushes[c, slot].start()

    there = pl.ds(pl.multiple_of((1 - h) * 128, 128), 128)
    for c in ORDER:
        came = w.at[c, z, g, :, there]
        push(came, came, hx_s.at[c], hx_r.at[c], at_h).wait_recv()
        block = w.at[c, z, g]
        for way, where in ((0, at_z_up), (1, at_z_down)):
            z_pushes[c, way] = push(block, block, z_s.at[c, way], z_r.at[c, way], where)
            z_pushes[c, way].start()
        share(c, 0, z)

    fwd_pushes = []
    half = PIECES // 2
    for p in range(half):
        for way, source, where, piece in ((0, y_down, at_y_up, p), (1, y_up, at_y_down, p + half)):
            block = raw.at[source, pl.ds(piece * PIECE, PIECE), :]
            push(block, block, tok_s.at[way, piece], tok_r.at[way, piece], where).wait_recv()
            copy = push(block, block, fwd_s.at[way, p], fwd_r.at[way, p], where)
            copy.start()
            fwd_pushes.append(copy)
    for p in range(half):
        for way, source, where, piece in ((0, y_down, at_y_up, p + half), (1, y_up, at_y_down, p)):
            block = raw.at[source, pl.ds(piece * PIECE, PIECE), :]
            push(block, block, tok_s.at[way, piece], tok_r.at[way, piece], where).wait_recv()
    normalize(y_down)
    normalize(y_up)

    for c in ORDER:
        for way, source, where in ((0, z_down, at_z_up), (1, z_up, at_z_down)):
            came = w.at[c, source, g]
            push(came, came, z_s.at[c, way], z_r.at[c, way], where).wait_recv()
            block = w.at[c, source, g, :, pl.ds(way * 128, 128)]
            zf_pushes[c, way] = push(block, block, zf_s.at[c, way], zf_r.at[c, way], where)
            zf_pushes[c, way].start()
            share(c, 1 + way, source)

    for p in range(half):
        for way, where, piece in ((0, at_y_up, p), (1, at_y_down, p + half)):
            block = raw.at[y_far, pl.ds(piece * PIECE, PIECE), :]
            push(block, block, fwd_s.at[way, p], fwd_r.at[way, p], where).wait_recv()
    normalize(y_far)

    def multiply(c, panel, out):
        def step(i, carry):
            rows = pl.ds(pl.multiple_of(i * 512, 512), 512)
            total = jnp.dot(normed[0, rows, :], w[c, 0, panel], preferred_element_type=F32)
            for block in range(1, 4):
                total = total + jnp.dot(normed[block, rows, :], w[c, block, panel], preferred_element_type=F32)
            out[c, rows, :] = total.astype(out.dtype)
            return carry

        lax.fori_loop(0, TOK // 512, step, 0)

    def finish(c):
        ps_pushes[c].wait_recv()

        def step(i, carry):
            rows = pl.ds(pl.multiple_of(i * 64, 64), 64)
            pair = (own[c, rows, :] + ps_in[c, rows, :].astype(F32)) * D ** (-0.5)
            for head, values in ((c, pair[:, 0:128]), (3 + c, pair[:, 128:256])):
                if head < 5:
                    turned = jnp.concatenate([values[:, 64:], values[:, :64]], axis=1)
                    values = values * table_ref[0, rows, :] + turned * table_ref[1, rows, :]
                qkv_ref[head, rows, :] = values.astype(BF16)
            return carry

        lax.fori_loop(0, TOK // 64, step, 0)

    ps_pushes = [None] * 3
    for place, c in enumerate(ORDER):
        for way, where in ((0, at_z_up), (1, at_z_down)):
            came = w.at[c, z_far, g, :, pl.ds(way * 128, 128)]
            push(came, came, zf_s.at[c, way], zf_r.at[c, way], where).wait_recv()
        share(c, 3, z_far)
        for slot, source in enumerate((z, z_down, z_up, z_far)):
            came = w.at[c, source, 1 - g]
            push(came, came, sib_s.at[c, slot], sib_r.at[c, slot], at_core).wait_recv()
        multiply(c, 1 - l, ps_out)
        ps_pushes[c] = push(ps_out.at[c], ps_in.at[c], ps_s.at[c], ps_r.at[c], at_x)
        ps_pushes[c].start()
        multiply(c, l, own)
        if place > 0:
            finish(ORDER[place - 1])
    finish(ORDER[-1])

    for copy in tok_pushes + fwd_pushes + a_pushes + b_pushes + hx_pushes + ps_pushes:
        copy.wait_send()
    for copies in (z_pushes, zf_pushes, sib_pushes):
        for copy in copies.values():
            copy.wait_send()

    @pl.when(holds_prior)
    def _():
        prior_push.wait_send()

    @pl.when(jnp.logical_not(straight))
    def _():
        for c in range(3):
            s1_pushes[c].wait_send()


def project(master, moment, second, gradient, prior, tokens, gain, tables):
    dma = pltpu.SemaphoreType.DMA
    vmem = pl.BlockSpec(memory_space=pltpu.VMEM)
    hbm = pl.BlockSpec(memory_space=pl.ANY)
    return pl.pallas_call(
        project_kernel,
        out_shape=(
            jax.ShapeDtypeStruct((QPK + 2, TOK, HD), BF16),
            jax.ShapeDtypeStruct((8, 128), F32),
        ),
        in_specs=[hbm] * 6 + [vmem] * 2,
        out_specs=(vmem, vmem),
        scratch_shapes=[
            pltpu.VMEM((4, TOK, FEAT), BF16),
            pltpu.VMEM((4, TOK, FEAT), BF16),
            pltpu.VMEM((3, 4, 2, FEAT, 256), BF16),
            pltpu.VMEM((FEAT, COLS), F32),
            pltpu.VMEM((FEAT, COLS), F32),
            pltpu.VMEM((FEAT, COLS), F32),
            pltpu.VMEM((FEAT, COLS), BF16),
            pltpu.VMEM((TOK, 128), F32),
            pltpu.VMEM((8, 16, 128), F32),
            pltpu.VMEM((16, 8, 128), F32),
            pltpu.VMEM((3, FEAT, 128), BF16),
            pltpu.VMEM((3, FEAT, 128), BF16),
            pltpu.VMEM((FEAT, COLS), BF16),
            pltpu.VMEM((3, TOK, 256), F32),
            pltpu.VMEM((3, TOK, 256), SUM_TYPE),
            pltpu.VMEM((3, TOK, 256), SUM_TYPE),
            dma((6,)),
            dma((2, PIECES)), dma((2, PIECES)), dma((2, PIECES // 2)), dma((2, PIECES // 2)),
            dma((7,)), dma((7,)), dma((15,)), dma((15,)),
            dma, dma, dma((3,)), dma((3,)), dma((3,)), dma((3,)),
            dma((3, 2)), dma((3, 2)), dma((3, 2)), dma((3, 2)),
            dma((3, 4)), dma((3, 4)), dma((3,)), dma((3,)),
        ],
        compiler_params=pltpu.CompilerParams(
            collective_id=0, has_side_effects=True, vmem_limit_bytes=60 * 1024 * 1024
        ),
        cost_estimate=pl.CostEstimate(
            flops=2 * TOK * D * 768, bytes_accessed=24 * 1024 * 1024, transcendentals=0
        ),
    )(master, moment, second, gradient, prior, tokens, gain, tables)


BLOCK = 256


def attend_kernel(
    qkv_ref, clip_ref, seg_ref, master_ref, moment_ref, second_ref, grad_ref,
    new_master_ref, new_moment_ref, new_second_ref, out_ref,
):
    place = pl.program_id(0)

    def adam_rows(i, carry):
        rows = pl.ds(pl.multiple_of(i * 32, 32), 32)
        clip = jnp.concatenate([clip_ref[0:1, :]] * 3, axis=1)
        new_master, new_moment, new_second = adam(
            master_ref[rows, :], moment_ref[rows, :], second_ref[rows, :], grad_ref[rows, :].astype(F32), clip
        )
        new_master_ref[rows, :] = new_master
        new_moment_ref[rows, :] = new_moment
        new_second_ref[rows, :] = new_second
        return carry

    lax.fori_loop(0, BLOCK // 32, adam_rows, 0)

    for q in range(TOK // BLOCK):
        @pl.when(place == q)
        def _(q=q):
            first = max(0, q - 2) * BLOCK
            last = (q + 1) * BLOCK
            width = last - first
            segments = seg_ref[0:1, :].astype(F32)
            column = jnp.concatenate(
                [
                    jnp.broadcast_to(segments[:, s:s + 128], (128, 128)).T
                    for s in range(q * BLOCK, last, 128)
                ],
                axis=0,
            )
            same = jnp.concatenate([column] * (width // 128), axis=1) == segments[:, first:last]
            at_query = lax.broadcasted_iota(jnp.int32, (BLOCK, width), 0) + q * BLOCK
            at_key = lax.broadcasted_iota(jnp.int32, (BLOCK, width), 1) + first
            allowed = same & (at_query >= at_key)
            for head in range(QPK):
                scores = lax.dot_general(
                    qkv_ref[head, q * BLOCK:last, :], qkv_ref[QPK, first:last, :],
                    (((1,), (1,)), ((), ())), preferred_element_type=F32,
                ) * HD ** (-0.5)
                scores = jnp.where(allowed, scores, -jnp.inf)
                weights = jnp.exp(scores - jnp.max(scores, axis=1, keepdims=True))
                weights = (weights / jnp.sum(weights, axis=1, keepdims=True)).astype(BF16)
                out_ref[:, head * HD:(head + 1) * HD] = jnp.dot(
                    weights, qkv_ref[QPK + 1, first:last, :], preferred_element_type=F32
                ).astype(BF16)


def attend(qkv, clip, segments, master, moment, second, gradient):
    steps = TOK // BLOCK
    rows = pl.BlockSpec((BLOCK, COLS), lambda i: (i, 0))
    return pl.pallas_call(
        attend_kernel,
        grid=(steps,),
        out_shape=(
            jax.ShapeDtypeStruct((FEAT, COLS), F32),
            jax.ShapeDtypeStruct((FEAT, COLS), F32),
            jax.ShapeDtypeStruct((FEAT, COLS), F32),
            jax.ShapeDtypeStruct((TOK, QPK * HD), BF16),
        ),
        in_specs=[
            pl.BlockSpec((QPK + 2, TOK, HD), lambda i: (0, 0, 0)),
            pl.BlockSpec((8, 128), lambda i: (0, 0)),
            pl.BlockSpec((1, TOK), lambda i: (0, 0)),
            rows, rows, rows, rows,
        ],
        out_specs=(rows, rows, rows, pl.BlockSpec((BLOCK, QPK * HD), lambda i: (i, 0))),
        compiler_params=pltpu.CompilerParams(vmem_limit_bytes=48 * 1024 * 1024),
    )(qkv, clip, segments, master, moment, second, gradient)


def shards(master, moment, second, gradient, prior_weights, tokens, norm_gain, segment_ids):
    qkv, clip = project(
        master, moment, second, gradient, prior_weights, tokens[0], norm_gain.reshape(8, 1, FEAT),
        jnp.asarray(rotary_tables()),
    )
    new_master, new_moment, new_second, attended = attend(
        qkv, clip, segment_ids, master, moment, second, gradient
    )
    return (new_master, new_moment, new_second, attended[None])


def solution(mesh):
    in_specs = (
        P("tensor", ("group", "fsdp")),
        P("tensor", ("group", "fsdp")),
        P("tensor", ("group", "fsdp")),
        P("tensor", ("group", "fsdp")),
        P(None, "tensor"),
        P(("group", "fsdp"), None, "tensor"),
        P(),
        P(("group", "fsdp"), None),
    )
    out_specs = (
        P("tensor", ("group", "fsdp")),
        P("tensor", ("group", "fsdp")),
        P("tensor", ("group", "fsdp")),
        P(("group", "fsdp"), None, "tensor"),
    )
    return jax.shard_map(shards, mesh=mesh, in_specs=in_specs, out_specs=out_specs, check_vma=False)
```

time: 919 us -> 200 us (0.22)
  waiting for transfers between devices: 752 us -> 0 us
  Pallas kernels: 0 us -> 197 us
  blocking collectives: 82.2 us -> 0 us
  other arithmetic: 31.3 us -> 0 us
  matrix products: 29.4 us -> 0 us
  between operations: 14.6 us -> 0.71 us
    psum x1 -> x0, waiting for transfers between devices: 511 us -> none  [spread(): return lax.psum(block, axis)]
    all_gather x2 -> x0, waiting for transfers between devices: 241 us -> none  [the longest x1 172 us: shards(): normed = lax.all_gather(normed_part, 'tensor', axis=1, tiled=True)]
    pallas_call x0 -> x2, Pallas kernels: none -> 197 us  [the longest x1 185 us: project(): pl.pallas_call(project_kernel, out_shape=(jax.ShapeDtypeStruct((QPK + 2,...]
    psum x2 -> x0, blocking collectives: 82.2 us -> none  [the longest x1 68.7 us: shards(): overall = lax.psum(local_sq, ('group', 'fsdp', 'tensor'))]
    dot_general x3 -> x0, matrix products: 29.4 us -> none  [the longest x1 19 us: shards(): jnp.dot(normed, mixed_panel, preferred_element_type=jnp.float32)]
  transfers between devices with their start and end apart: 3 -> 0, of which waited for: 3 -> 0; matrix products, arithmetic and copies ran while one was open for 1% -> 0% of each run, Pallas kernels for 0% -> 0%
where the time goes in v1:
time: 200 us
  Pallas kernels  197 us (98%)
  local copies, waits for them, and re-layouts  2.1 us (1%)
    pallas_call x1, Pallas kernels, project(): pl.pallas_call(project_kernel, out_shape=(jax.ShapeDtypeStruct((QPK + 2,...  185 us
    pallas_call x1, Pallas kernels, attend(): pl.pallas_call(attend_kernel, grid=(steps,), out_shape=(jax.ShapeDtypeStr...  11.7 us

profile of v1, /device:TPU:1, one launch (start us, length us, event | category | flops | bytes accessed | tf_op | source)
XLA Modules:
  0.0 199.6 jit_solution(8425180473265312743)
XLA Ops:
  0.6 0.0 copy-start
  0.6 0.0 copy-start.1
  0.7 0.0 copy-start.3
  0.7 0.0 copy-start.4
  0.7 185.1 %shard_map.120 = (bf16[6,1024,128]{2,1,0:T(8,128)(2,1)}, f32[8,128]{1,0:T(8,128)}) custom-call(f32[1024,384]{1,0:T(8,128)} %master_ref.3, f32[1024,384]{1,0:T(8,128)} %moment_ref.3, f32[1024,384]{1,0:T(8,128)} %second_ref.3, bf16[1024,384]{1,0:T(8,128)(2,1)} %grad_ref.3, bf16[8192,768]{1,0:T(8,128)(2,1)} %prior_ref.1, bf16[1024,1024]{1,0:T(8,128)(2,1)} %bitcast.3, ...), custom_call_target="tpu_custom_call" | custom-call | flops 12884901888 | bytes 25165824 | tf_op jit(solution)/shard_map/pallas_call | solution.py:361
  185.7 0.0 copy-done
  185.8 0.0 copy-done.1
  185.8 0.0 copy-done.3
  185.8 0.0 copy-done.4
  185.8 0.0 copy-start.2
  185.8 1.4 copy-done.2
  187.2 0.0 copy-start.5
  187.2 0.7 copy-done.5
  187.9 11.7 %shard_map.121 = (f32[1024,384]{1,0:T(8,128)}, f32[1024,384]{1,0:T(8,128)}, f32[1024,384]{1,0:T(8,128)}, bf16[1024,512]{1,0:T(8,128)(2,1)}) custom-call(bf16[6,1024,128]{2,1,0:T(8,128)(2,1)S(1)} %copy-done.2, f32[8,128]{1,0:T(8,128)S(1)} %copy-done.5, s32[1,1024]{1,0:T(1,128)S(1)} %copy-done.4, f32[1024,384]{1,0:T(8,128)S(1)} %copy-done, ...), custom_call_target="tpu_custom_call" | custom-call | tf_op jit(solution)/shard_map/pallas_call | solution.py:458
Async XLA Ops:
  0.6 185.1 %copy-start = (f32[1024,384]{1,0:T(8,128)S(1)}, f32[1024,384]{1,0:T(8,128)}, u32[]{:S(2)}) copy-start(f32[1024,384]{1,0:T(8,128)} %master_ref.3) | copy-start | bytes 4718596
  0.6 185.1 %copy-start.1 = (f32[1024,384]{1,0:T(8,128)S(1)}, f32[1024,384]{1,0:T(8,128)}, u32[]{:S(2)}) copy-start(f32[1024,384]{1,0:T(8,128)} %moment_ref.3) | copy-start | bytes 4718596
  0.7 185.1 %copy-start.3 = (bf16[1024,384]{1,0:T(8,128)(2,1)S(1)}, bf16[1024,384]{1,0:T(8,128)(2,1)}, u32[]{:S(2)}) copy-start(bf16[1024,384]{1,0:T(8,128)(2,1)} %grad_ref.3) | copy-start | bytes 2359300
  0.7 185.1 %copy-start.4 = (s32[1,1024]{1,0:T(1,128)S(1)}, s32[1,1024]{1,0:T(1,128)}, u32[]{:S(2)}) copy-start(s32[1,1024]{1,0:T(1,128)} %seg_ref.1) | copy-start | bytes 12292
  185.8 1.4 copy-start.2
  187.2 0.7 copy-start.5

commit v2 on v1

v2 whole, which is shorter than its diff:
```python
import functools
import math

import jax
import jax.numpy as jnp
import numpy as np
from jax import lax
from jax.experimental import pallas as pl
from jax.experimental.pallas import tpu as pltpu
from jax.sharding import PartitionSpec as P

D = 8192
HD = 128
QPK = 4
QKV = 6144

learn_rate = 0.01
decay_rate = 0.1
clip_rms = 0.25
first_fix = 1.0 - math.exp(200.0 * math.log(0.9))
second_fix = 1.0 - math.exp(200.0 * math.log(0.95))
mix_share = 0.6

MESH = pl.DeviceIdType.MESH
F32 = jnp.float32
BF16 = jnp.bfloat16
SUM_TYPE = BF16
TOK = 1024
FEAT = 1024
COLS = 384
PIECES = 8
PIECE = TOK // PIECES
ORDER = (2, 1, 0)


def rotary_tables():
    places = np.arange(TOK).astype(np.float32)
    lanes = np.arange(HD // 2).astype(np.float32)
    frequencies = np.power(500000.0, -(lanes * np.float32(2.0) / np.float32(HD)).astype(np.float64))
    angles = places[:, None] * frequencies.astype(np.float32)[None, :]
    cosine = np.cos(angles.astype(np.float64)).astype(np.float32)
    sine = np.sin(angles.astype(np.float64)).astype(np.float32)
    return np.stack(
        [np.concatenate([cosine, cosine], 1), np.concatenate([-sine, sine], 1)]
    ).astype(np.float32)


def adam(master, moment, second, grad, clip):
    clipped = clip * grad
    new_moment = 0.9 * moment + 0.1 * clipped
    new_second = 0.95 * second + 0.05 * clipped * clipped
    update = (
        new_moment / first_fix / (jnp.sqrt(new_second / second_fix) + 1e-08) + decay_rate * master
    )
    return master - learn_rate * update, new_moment, new_second


def push(src, dst, send, recv, where):
    return pltpu.make_async_remote_copy(
        src_ref=src, dst_ref=dst, send_sem=send, recv_sem=recv, device_id=where, device_id_type=MESH
    )


def project_kernel(
    master_ref, moment_ref, second_ref, grad_ref, prior_ref, tok_ref, gain_ref, table_ref,
    qkv_ref, clip_ref,
    raw, normed, w, mas, mom, sec, gra, inv, msg_a, msg_b, msg_r, z_out, z_in, y_in, pri, own, ps_out, ps_in,
    load_sem, tok_s, tok_r, fwd_s, fwd_r, a_s, a_r, b_s, b_r, r_s, r_r, pri_s, pri_r,
    za_s, za_r, ya_s, ya_r, hx_s, hx_r, zg_s, zg_r, zf_s, zf_r, sib_s, sib_r, ps_s, ps_r,
):
    g = lax.axis_index("group")
    f = lax.axis_index("fsdp")
    t = lax.axis_index("tensor")
    z, h = f // 2, f % 2
    l, y = t // 4, t % 4
    y_up, y_down, y_far = (y + 1) % 4, (y + 3) % 4, (y + 2) % 4
    z_up, z_down, z_far = (z + 1) % 4, (z + 3) % 4, (z + 2) % 4
    at_y_up, at_y_down = (g, f, l * 4 + y_up), (g, f, l * 4 + y_down)
    at_z_up, at_z_down = (g, z_up * 2 + h, t), (g, z_down * 2 + h, t)
    at_x = (g, f, (1 - l) * 4 + y)
    at_h = (g, z * 2 + (1 - h), t)
    at_core = (1 - g, f, t)
    mine = g * 8 + f
    quarter = (z + 4 - y) % 4
    quarter_up, quarter_down, quarter_far = (quarter + 1) % 4, (quarter + 3) % 4, (quarter + 2) % 4

    loads = [
        pltpu.make_async_copy(grad_ref, gra, load_sem.at[0]),
        pltpu.make_async_copy(tok_ref, raw.at[y], load_sem.at[1]),
        pltpu.make_async_copy(master_ref, mas, load_sem.at[2]),
        pltpu.make_async_copy(moment_ref, mom, load_sem.at[3]),
        pltpu.make_async_copy(second_ref, sec, load_sem.at[4]),
    ]
    for load in loads:
        load.start()
    prior_cols = pl.ds(pl.multiple_of(h * COLS, 128), COLS)
    prior_here = pltpu.make_async_copy(
        prior_ref.at[pl.ds(l * 4, 4), quarter, :, prior_cols], pri, load_sem.at[5]
    )
    prior_push = push(
        prior_ref.at[pl.ds((1 - l) * 4, 4), quarter, :, prior_cols], pri, pri_s, pri_r, at_x
    )
    holds_prior = g == l

    peers_a = [(g, f, (t + d) % 8) for d in range(1, 8)]
    places_b = [(mine + d) % 16 for d in range(1, 16)]
    peers_b = [(place // 8, place % 8, t) for place in places_b]

    barrier = pltpu.get_barrier_semaphore()
    for peer in peers_a + peers_b:
        pl.semaphore_signal(barrier, inc=1, device_id=peer, device_id_type=MESH)

    loads[0].wait()

    def grad_sum(i, total):
        v = gra[pl.ds(pl.multiple_of(i * 64, 64), 64), :].astype(F32)
        return total + jnp.sum((v * v).reshape(8, 8, COLS), axis=0)

    total = lax.fori_loop(0, FEAT // 64, grad_sum, jnp.zeros((8, COLS), F32))
    msg_a[t] = total[:, 0:128] + total[:, 128:256] + total[:, 256:384]
    pl.semaphore_wait(barrier, 22)

    def send_all(msg, slot, send, recv, peers):
        copies = [push(msg.at[slot], msg.at[slot], send.at[d], recv.at[d], peer) for d, peer in enumerate(peers)]
        for copy in copies:
            copy.start()
        return copies

    def wait_all(msg, slot, send, recv, peers):
        count = len(peers) + 1
        for d, peer in enumerate(peers):
            source = (slot + count - 1 - d) % count
            push(msg.at[source], msg.at[source], send.at[d], recv.at[d], peer).wait_recv()
        sums = msg[0]
        for s in range(1, count):
            sums = sums + msg[s]
        return sums

    a_pushes = send_all(msg_a, t, a_s, a_r, peers_a)

    tok_pushes = []

    def tok_rows(piece):
        return pl.ds(piece * PIECE, PIECE)

    def own_pair(j):
        for piece in (2 * j, 2 * j + 1):
            for way, where in ((0, at_y_up), (1, at_y_down)):
                copy = push(
                    tok_ref.at[tok_rows(piece), :], raw.at[y, tok_rows(piece), :],
                    tok_s.at[way, piece], tok_r.at[way, piece], where,
                )
                copy.start()
                tok_pushes.append(copy)

    def forward_pair(j):
        for way, source, where in ((0, y_down, at_y_up), (1, y_up, at_y_down)):
            piece = 2 * j + way
            block = raw.at[source, tok_rows(piece), :]
            push(block, block, tok_s.at[way, piece], tok_r.at[way, piece], where).wait_recv()
            copy = push(block, block, fwd_s.at[way, j], fwd_r.at[way, j], where)
            copy.start()
            tok_pushes.append(copy)

    def normalize(block, j):
        gain = gain_ref[l * 4 + block]
        cols = pl.ds(pl.multiple_of(block * FEAT, FEAT), FEAT)

        def step(i, carry):
            rows = pl.ds(pl.multiple_of(j * 256 + i * 32, 32), 32)
            scale = jnp.concatenate([inv[rows, :]] * (FEAT // 128), axis=1)
            normed[rows, cols] = (raw[block, rows, :].astype(F32) * scale * gain).astype(BF16)
            return carry

        lax.fori_loop(0, 8, step, 0)

    def ready_pair(j):
        for way, source, where in ((0, y_down, at_y_up), (1, y_up, at_y_down)):
            piece = 2 * j + 1 - way
            block = raw.at[source, tok_rows(piece), :]
            push(block, block, tok_s.at[way, piece], tok_r.at[way, piece], where).wait_recv()
        normalize(y_down, j)
        normalize(y_up, j)
        for way, where in ((0, at_y_up), (1, at_y_down)):
            block = raw.at[y_far, tok_rows(2 * j + way), :]
            push(block, block, fwd_s.at[way, j], fwd_r.at[way, j], where).wait_recv()
        normalize(y_far, j)

    own_pair(0)

    @pl.when(holds_prior)
    def _():
        prior_push.start()
        prior_here.start()

    loads[1].wait()
    for i in range(8):
        part = jnp.zeros((128, 128), F32)
        for j in range(FEAT // 128):
            v = raw[y, i * 128:(i + 1) * 128, j * 128:(j + 1) * 128].astype(F32)
            part = part + v * v
        msg_r[t, i:i + 1, :] = jnp.sum(part.T, axis=0, keepdims=True)

    msg_b[mine] = wait_all(msg_a, t, a_s, a_r, peers_a)
    b_pushes = send_all(msg_b, mine, b_s, b_r, peers_b)
    r_pushes = send_all(msg_r, t, r_s, r_r, peers_a)
    sums = wait_all(msg_b, mine, b_s, b_r, peers_b)
    overall = jnp.broadcast_to(jnp.sum(sums, keepdims=True), (8, 128))
    clip_ref[...] = jnp.minimum(1.0, clip_rms * math.sqrt(D * QKV) / (jnp.sqrt(overall) + 1e-06))

    for load in loads[2:]:
        load.wait()
    za_pushes, ya_pushes, hx_pushes, zg_pushes, zf_pushes, sib_pushes, ps_pushes = {}, {}, {}, {}, {}, {}, {}

    def update(c):
        cols = slice(c * 128, (c + 1) * 128)

        def step(i, carry):
            rows = pl.ds(pl.multiple_of(i * 64, 64), 64)
            updated, _, _ = adam(
                mas[rows, cols], mom[rows, cols], sec[rows, cols], gra[rows, cols].astype(F32), clip_ref[0:1, :]
            )
            z_out[c, i // 4, pl.ds(pl.multiple_of(i % 4 * 64, 64), 64), :] = updated.astype(BF16)
            return carry

        lax.fori_loop(0, FEAT // 64, step, 0)
        for d in range(1, 4):
            za_pushes[c, d] = push(
                z_out.at[c, d], z_in.at[c, d], za_s.at[c, d - 1], za_r.at[c, d - 1], (g, (z + d) % 4 * 2 + h, t)
            )
            za_pushes[c, d].start()
        z_in[c, 0] = z_out[c, 0]

    def deal(c):
        for d in range(1, 4):
            za_pushes[c, d].wait_recv()
        for d in range(1, 4):
            other = (y + d) % 4
            ya_pushes[c, d] = push(
                z_in.at[c, (z + 4 - other) % 4], y_in.at[c, y], ya_s.at[c, d - 1], ya_r.at[c, d - 1],
                (g, f, l * 4 + other),
            )
            ya_pushes[c, d].start()
        y_in[c, y] = z_in[c, quarter]

    here = pl.ds(pl.multiple_of(h * 128, 128), 128)
    there = pl.ds(pl.multiple_of((1 - h) * 128, 128), 128)

    def part_of(c, q, cols):
        return w.at[c, :, g, q, :, cols]

    def mix(c):
        for d in range(1, 4):
            block = y_in.at[c, (y + 4 - d) % 4]
            push(block, block, ya_s.at[c, d - 1], ya_r.at[c, d - 1], (g, f, l * 4 + (y + d) % 4)).wait_recv()
        for block in range(4):
            policy = y_in[c, block].astype(F32)
            prior = pri[block, :, c * 128:(c + 1) * 128].astype(F32)
            w[c, block, g, quarter, :, here] = (mix_share * policy + (1.0 - mix_share) * prior).astype(BF16)
        block = part_of(c, quarter, here)
        hx_pushes[c] = push(block, block, hx_s.at[c], hx_r.at[c], at_h)
        hx_pushes[c].start()

    def along_z(c, part):
        block = part_of(c, quarter, (here, there)[part])
        for way, where in ((0, at_z_up), (1, at_z_down)):
            zg_pushes[c, part, way] = push(block, block, zg_s.at[c, part, way], zg_r.at[c, part, way], where)
            zg_pushes[c, part, way].start()

    def share(c, slot, q):
        block = w.at[c, :, g, q]
        sib_pushes[c, slot] = push(block, block, sib_s.at[c, slot], sib_r.at[c, slot], at_core)
        sib_pushes[c, slot].start()

    def across(c):
        came = part_of(c, quarter, there)
        push(came, came, hx_s.at[c], hx_r.at[c], at_h).wait_recv()

    def onward(c):
        ways = ((0, quarter_down, at_z_up), (1, quarter_up, at_z_down))
        for part in range(2):
            for way, q, where in ways:
                block = part_of(c, q, (here, there)[part])
                push(block, block, zg_s.at[c, part, way], zg_r.at[c, part, way], where).wait_recv()
                if part == way:
                    zf_pushes[c, way] = push(block, block, zf_s.at[c, way], zf_r.at[c, way], where)
                    zf_pushes[c, way].start()
        for way, q, where in ways:
            share(c, 1 + way, q)

    def complete(c):
        for way, where in ((0, at_z_up), (1, at_z_down)):
            block = part_of(c, quarter_far, (here, there)[way])
            push(block, block, zf_s.at[c, way], zf_r.at[c, way], where).wait_recv()
        share(c, 3, quarter_far)
        for slot, q in enumerate((quarter, quarter_down, quarter_up, quarter_far)):
            block = w.at[c, :, 1 - g, q]
            push(block, block, sib_s.at[c, slot], sib_r.at[c, slot], at_core).wait_recv()

    def multiply(j, c):
        rows = pl.ds(j * 256, 256)

        def half(panel):
            return jnp.dot(
                normed[rows, :], w[c, :, panel].reshape(4 * FEAT, 256), preferred_element_type=F32
            )

        ps_out[c, j] = half(1 - l).astype(SUM_TYPE)
        ps_pushes[j, c] = push(ps_out.at[c, j], ps_in.at[c, j], ps_s.at[c, j], ps_r.at[c, j], at_x)
        ps_pushes[j, c].start()
        own[c, j] = half(l)

    def finish(j, c):
        ps_pushes[j, c].wait_recv()

        def step(i, carry):
            rows = pl.ds(pl.multiple_of(i * 64, 64), 64)
            at = pl.ds(pl.multiple_of(j * 256 + i * 64, 64), 64)
            pair = (own[c, j, rows, :] + ps_in[c, j, rows, :].astype(F32)) * D ** (-0.5)
            for head, values in ((c, pair[:, 0:128]), (3 + c, pair[:, 128:256])):
                if head < 5:
                    turned = jnp.concatenate([values[:, 64:], values[:, :64]], axis=1)
                    values = values * table_ref[0, at, :] + turned * table_ref[1, at, :]
                qkv_ref[head, at, :] = values.astype(BF16)
            return carry

        lax.fori_loop(0, 4, step, 0)

    first, second, third = ORDER
    for c in ORDER:
        update(c)
    own_pair(1)
    inverse = lax.rsqrt(wait_all(msg_r, t, r_s, r_r, peers_a) / D + 1e-05)
    for i in range(8):
        inv[i * 128:(i + 1) * 128, :] = jnp.broadcast_to(inverse[i:i + 1, :], (128, 128)).T
    for c in ORDER:
        deal(c)
    forward_pair(0)

    @pl.when(holds_prior)
    def _():
        prior_here.wait()

    @pl.when(jnp.logical_not(holds_prior))
    def _():
        prior_push.wait_recv()

    mix(first)
    along_z(first, 0)
    mix(second)
    mix(third)
    own_pair(2)
    across(first)
    along_z(first, 1)
    share(first, 0, quarter)
    along_z(second, 0)
    for j in range(4):
        normalize(y, j)
    forward_pair(1)
    across(second)
    along_z(second, 1)
    share(second, 0, quarter)
    onward(first)
    own_pair(3)
    across(third)
    along_z(third, 0)
    along_z(third, 1)
    share(third, 0, quarter)
    ready_pair(0)
    complete(first)
    multiply(0, first)
    forward_pair(2)
    ready_pair(1)
    multiply(1, first)
    onward(second)
    finish(0, first)
    finish(1, first)
    complete(second)
    multiply(0, second)
    multiply(1, second)
    forward_pair(3)
    onward(third)
    ready_pair(2)
    multiply(2, first)
    multiply(2, second)
    finish(0, second)
    finish(1, second)
    complete(third)
    multiply(0, third)
    multiply(1, third)
    multiply(2, third)
    finish(2, first)
    finish(2, second)
    ready_pair(3)
    for c in ORDER:
        multiply(3, c)
    for j in range(3):
        finish(j, third)
    for c in ORDER:
        finish(3, c)

    for copy in tok_pushes + a_pushes + b_pushes + r_pushes:
        copy.wait_send()
    for copies in (za_pushes, ya_pushes, hx_pushes, zg_pushes, zf_pushes, sib_pushes, ps_pushes):
        for copy in copies.values():
            copy.wait_send()

    @pl.when(holds_prior)
    def _():
        prior_push.wait_send()


def project(master, moment, second, gradient, prior, tokens, gain, tables):
    dma = pltpu.SemaphoreType.DMA
    vmem = pl.BlockSpec(memory_space=pltpu.VMEM)
    hbm = pl.BlockSpec(memory_space=pl.ANY)
    return pl.pallas_call(
        project_kernel,
        out_shape=(
            jax.ShapeDtypeStruct((QPK + 2, TOK, HD), BF16),
            jax.ShapeDtypeStruct((8, 128), F32),
        ),
        in_specs=[hbm] * 6 + [vmem] * 2,
        out_specs=(vmem, vmem),
        scratch_shapes=[
            pltpu.VMEM((4, TOK, FEAT), BF16),
            pltpu.VMEM((TOK, 4 * FEAT), BF16),
            pltpu.VMEM((3, 4, 2, 4, 256, 256), BF16),
            pltpu.VMEM((FEAT, COLS), F32),
            pltpu.VMEM((FEAT, COLS), F32),
            pltpu.VMEM((FEAT, COLS), F32),
            pltpu.VMEM((FEAT, COLS), BF16),
            pltpu.VMEM((TOK, 128), F32),
            pltpu.VMEM((8, 8, 128), F32),
            pltpu.VMEM((16, 8, 128), F32),
            pltpu.VMEM((8, 8, 128), F32),
            pltpu.VMEM((3, 4, 256, 128), BF16),
            pltpu.VMEM((3, 4, 256, 128), BF16),
            pltpu.VMEM((3, 4, 256, 128), BF16),
            pltpu.VMEM((4, 256, COLS), BF16),
            pltpu.VMEM((3, 4, 256, 256), F32),
            pltpu.VMEM((3, 4, 256, 256), SUM_TYPE),
            pltpu.VMEM((3, 4, 256, 256), SUM_TYPE),
            dma((6,)),
            dma((2, PIECES)), dma((2, PIECES)), dma((2, 4)), dma((2, 4)),
            dma((7,)), dma((7,)), dma((15,)), dma((15,)), dma((7,)), dma((7,)),
            dma, dma,
            dma((3, 3)), dma((3, 3)), dma((3, 3)), dma((3, 3)), dma((3,)), dma((3,)),
            dma((3, 2, 2)), dma((3, 2, 2)), dma((3, 2)), dma((3, 2)),
            dma((3, 4)), dma((3, 4)), dma((3, 4)), dma((3, 4)),
        ],
        compiler_params=pltpu.CompilerParams(
            collective_id=0, has_side_effects=True, vmem_limit_bytes=60 * 1024 * 1024
        ),
        cost_estimate=pl.CostEstimate(
            flops=2 * TOK * D * 768, bytes_accessed=24 * 1024 * 1024, transcendentals=0
        ),
    )(master, moment, second, gradient, prior.reshape(8, 4, 256, 768), tokens, gain, tables)


BLOCK = 256


def attend_kernel(
    qkv_ref, clip_ref, seg_ref, master_ref, moment_ref, second_ref, grad_ref,
    new_master_ref, new_moment_ref, new_second_ref, out_ref,
):
    place = pl.program_id(0)

    def adam_rows(i, carry):
        rows = pl.ds(pl.multiple_of(i * 32, 32), 32)
        clip = jnp.concatenate([clip_ref[0:1, :]] * 3, axis=1)
        new_master, new_moment, new_second = adam(
            master_ref[rows, :], moment_ref[rows, :], second_ref[rows, :], grad_ref[rows, :].astype(F32), clip
        )
        new_master_ref[rows, :] = new_master
        new_moment_ref[rows, :] = new_moment
        new_second_ref[rows, :] = new_second
        return carry

    lax.fori_loop(0, BLOCK // 32, adam_rows, 0)

    for q in range(TOK // BLOCK):
        @pl.when(place == q)
        def _(q=q):
            first = max(0, q - 2) * BLOCK
            last = (q + 1) * BLOCK
            width = last - first
            segments = seg_ref[0:1, :].astype(F32)
            column = jnp.concatenate(
                [
                    jnp.broadcast_to(segments[:, s:s + 128], (128, 128)).T
                    for s in range(q * BLOCK, last, 128)
                ],
                axis=0,
            )
            same = jnp.concatenate([column] * (width // 128), axis=1) == segments[:, first:last]
            at_query = lax.broadcasted_iota(jnp.int32, (BLOCK, width), 0) + q * BLOCK
            at_key = lax.broadcasted_iota(jnp.int32, (BLOCK, width), 1) + first
            allowed = same & (at_query >= at_key)
            for head in range(QPK):
                scores = lax.dot_general(
                    qkv_ref[head, q * BLOCK:last, :], qkv_ref[QPK, first:last, :],
                    (((1,), (1,)), ((), ())), preferred_element_type=F32,
                ) * HD ** (-0.5)
                scores = jnp.where(allowed, scores, -jnp.inf)
                weights = jnp.exp(scores - jnp.max(scores, axis=1, keepdims=True))
                weights = (weights / jnp.sum(weights, axis=1, keepdims=True)).astype(BF16)
                out_ref[:, head * HD:(head + 1) * HD] = jnp.dot(
                    weights, qkv_ref[QPK + 1, first:last, :], preferred_element_type=F32
                ).astype(BF16)


def attend(qkv, clip, segments, master, moment, second, gradient):
    steps = TOK // BLOCK
    rows = pl.BlockSpec((BLOCK, COLS), lambda i: (i, 0))
    return pl.pallas_call(
        attend_kernel,
        grid=(steps,),
        out_shape=(
            jax.ShapeDtypeStruct((FEAT, COLS), F32),
            jax.ShapeDtypeStruct((FEAT, COLS), F32),
            jax.ShapeDtypeStruct((FEAT, COLS), F32),
            jax.ShapeDtypeStruct((TOK, QPK * HD), BF16),
        ),
        in_specs=[
            pl.BlockSpec((QPK + 2, TOK, HD), lambda i: (0, 0, 0)),
            pl.BlockSpec((8, 128), lambda i: (0, 0)),
            pl.BlockSpec((1, TOK), lambda i: (0, 0)),
            rows, rows, rows, rows,
        ],
        out_specs=(rows, rows, rows, pl.BlockSpec((BLOCK, QPK * HD), lambda i: (i, 0))),
        compiler_params=pltpu.CompilerParams(vmem_limit_bytes=48 * 1024 * 1024),
    )(qkv, clip, segments, master, moment, second, gradient)


def shards(master, moment, second, gradient, prior_weights, tokens, norm_gain, segment_ids):
    qkv, clip = project(
        master, moment, second, gradient, prior_weights, tokens[0], norm_gain.reshape(8, 1, FEAT),
        jnp.asarray(rotary_tables()),
    )
    new_master, new_moment, new_second, attended = attend(
        qkv, clip, segment_ids, master, moment, second, gradient
    )
    return (new_master, new_moment, new_second, attended[None])


def solution(mesh):
    in_specs = (
        P("tensor", ("group", "fsdp")),
        P("tensor", ("group", "fsdp")),
        P("tensor", ("group", "fsdp")),
        P("tensor", ("group", "fsdp")),
        P(None, "tensor"),
        P(("group", "fsdp"), None, "tensor"),
        P(),
        P(("group", "fsdp"), None),
    )
    out_specs = (
        P("tensor", ("group", "fsdp")),
        P("tensor", ("group", "fsdp")),
        P("tensor", ("group", "fsdp")),
        P(("group", "fsdp"), None, "tensor"),
    )
    return jax.shard_map(shards, mesh=mesh, in_specs=in_specs, out_specs=out_specs, check_vma=False)
```

time: 200 us -> 144 us (0.72)
  Pallas kernels: 197 us -> 140 us
    pallas_call x1, Pallas kernels: 185 us -> 129 us  [project(): pl.pallas_call(project_kernel, out_shape=(jax.ShapeDtypeStruct((QPK + 2,...]
where the time goes in v2:
time: 144 us; the launch traced here: 143 us
  Pallas kernels  140 us (97%)
  local copies, waits for them, and re-layouts  2.1 us (1%)
    pallas_call x1, Pallas kernels, project(): pl.pallas_call(project_kernel, out_shape=(jax.ShapeDtypeStruct((QPK + 2,...  129 us
    pallas_call x1, Pallas kernels, attend(): pl.pallas_call(attend_kernel, grid=(steps,), out_shape=(jax.ShapeDtypeStr...  11.7 us

profile of v2, /device:TPU:1, one launch (start us, length us, event | category | flops | bytes accessed | tf_op | source)
XLA Modules:
  0.0 143.3 jit_solution(4663800269854696656)
XLA Ops:
  0.6 0.0 copy-start
  0.6 0.0 copy-start.1
  0.7 0.0 copy-start.3
  0.7 0.0 copy-start.4
  0.7 128.8 %shard_map.120 = (bf16[6,1024,128]{2,1,0:T(8,128)(2,1)}, f32[8,128]{1,0:T(8,128)}) custom-call(f32[1024,384]{1,0:T(8,128)} %master_ref.3, f32[1024,384]{1,0:T(8,128)} %moment_ref.3, f32[1024,384]{1,0:T(8,128)} %second_ref.3, bf16[1024,384]{1,0:T(8,128)(2,1)} %grad_ref.3, bf16[8,4,256,768]{3,2,1,0:T(8,128)(2,1)} %bitcast.4, bf16[1024,1024]{1,0:T(8,128)(2,1)} %bitcast.5, ...), custom_call_target="tpu_custom_call" | custom-call | flops 12884901888 | bytes 25165824 | tf_op jit(solution)/shard_map/pallas_call | solution.py:417
  129.4 0.0 copy-done
  129.5 0.0 copy-done.1
  129.5 0.0 copy-done.3
  129.5 0.0 copy-done.4
  129.5 0.0 copy-start.2
  129.5 1.4 copy-done.2
  130.9 0.0 copy-start.5
  130.9 0.7 copy-done.5
  131.6 11.7 %shard_map.121 = (f32[1024,384]{1,0:T(8,128)}, f32[1024,384]{1,0:T(8,128)}, f32[1024,384]{1,0:T(8,128)}, bf16[1024,512]{1,0:T(8,128)(2,1)}) custom-call(bf16[6,1024,128]{2,1,0:T(8,128)(2,1)S(1)} %copy-done.2, f32[8,128]{1,0:T(8,128)S(1)} %copy-done.5, s32[1,1024]{1,0:T(1,128)S(1)} %copy-done.4, f32[1024,384]{1,0:T(8,128)S(1)} %copy-done, ...), custom_call_target="tpu_custom_call" | custom-call | tf_op jit(solution)/shard_map/pallas_call | solution.py:517
Async XLA Ops:
  0.6 128.8 %copy-start = (f32[1024,384]{1,0:T(8,128)S(1)}, f32[1024,384]{1,0:T(8,128)}, u32[]{:S(2)}) copy-start(f32[1024,384]{1,0:T(8,128)} %master_ref.3) | copy-start | bytes 4718596
  0.6 128.8 %copy-start.1 = (f32[1024,384]{1,0:T(8,128)S(1)}, f32[1024,384]{1,0:T(8,128)}, u32[]{:S(2)}) copy-start(f32[1024,384]{1,0:T(8,128)} %moment_ref.3) | copy-start | bytes 4718596
  0.7 128.8 %copy-start.3 = (bf16[1024,384]{1,0:T(8,128)(2,1)S(1)}, bf16[1024,384]{1,0:T(8,128)(2,1)}, u32[]{:S(2)}) copy-start(bf16[1024,384]{1,0:T(8,128)(2,1)} %grad_ref.3) | copy-start | bytes 2359300
  0.7 128.8 %copy-start.4 = (s32[1,1024]{1,0:T(1,128)S(1)}, s32[1,1024]{1,0:T(1,128)}, u32[]{:S(2)}) copy-start(s32[1,1024]{1,0:T(1,128)} %seg_ref.1) | copy-start | bytes 12292
  129.5 1.4 copy-start.2
  130.9 0.7 copy-start.5

commit v3 on v2

--- a/solution.py
+++ b/solution.py
@@ -62,9 +62,9 @@
 
 
 def project_kernel(
-    master_ref, moment_ref, second_ref, grad_ref, prior_ref, tok_ref, gain_ref, table_ref,
-    qkv_ref, clip_ref,
-    raw, normed, w, mas, mom, sec, gra, inv, msg_a, msg_b, msg_r, z_out, z_in, y_in, pri, own, ps_out, ps_in,
+    master_ref, moment_ref, second_ref, grad_ref, prior_ref, tok_ref, gain_ref, table_ref, seg_ref,
+    out_ref, clip_ref,
+    raw, normed, w, mas, mom, sec, gra, inv, msg_a, msg_b, msg_r, z_out, z_in, y_in, pri, own, ps_out, ps_in, qkv, bias,
     load_sem, tok_s, tok_r, fwd_s, fwd_r, a_s, a_r, b_s, b_r, r_s, r_r, pri_s, pri_r,
     za_s, za_r, ya_s, ya_r, hx_s, hx_r, zg_s, zg_r, zf_s, zf_r, sib_s, sib_r, ps_s, ps_r,
 ):
@@ -186,13 +186,6 @@
             push(block, block, fwd_s.at[way, j], fwd_r.at[way, j], where).wait_recv()
         normalize(y_far, j)
 
-    own_pair(0)
-
-    @pl.when(holds_prior)
-    def _():
-        prior_push.start()
-        prior_here.start()
-
     loads[1].wait()
     for i in range(8):
         part = jnp.zeros((128, 128), F32)
@@ -203,7 +196,7 @@
 
     msg_b[mine] = wait_all(msg_a, t, a_s, a_r, peers_a)
     b_pushes = send_all(msg_b, mine, b_s, b_r, peers_b)
-    r_pushes = send_all(msg_r, t, r_s, r_r, peers_a)
+    own_pair(0)
     sums = wait_all(msg_b, mine, b_s, b_r, peers_b)
     overall = jnp.broadcast_to(jnp.sum(sums, keepdims=True), (8, 128))
     clip_ref[...] = jnp.minimum(1.0, clip_rms * math.sqrt(D * QKV) / (jnp.sqrt(overall) + 1e-06))
@@ -321,83 +314,141 @@
                 if head < 5:
                     turned = jnp.concatenate([values[:, 64:], values[:, :64]], axis=1)
                     values = values * table_ref[0, at, :] + turned * table_ref[1, at, :]
-                qkv_ref[head, at, :] = values.astype(BF16)
+                qkv[head, at, :] = values.astype(BF16)
             return carry
 
         lax.fori_loop(0, 4, step, 0)
 
+    def key_range(j):
+        return max(0, j - 2) * 256, (j + 1) * 256
+
+    def mask(j):
+        low, high = key_range(j)
+        segments = seg_ref[0:1, :].astype(F32)
+        column = jnp.concatenate(
+            [
+                jnp.broadcast_to(segments[:, s:s + 128], (128, 128)).T
+                for s in range(j * 256, high, 128)
+            ],
+            axis=0,
+        )
+        same = jnp.concatenate([column] * ((high - low) // 128), axis=1) == segments[:, low:high]
+        at_query = lax.broadcasted_iota(jnp.int32, (256, high - low), 0) + j * 256
+        at_key = lax.broadcasted_iota(jnp.int32, (256, high - low), 1) + low
+        bias[j, :, 0:high - low] = jnp.where(same & (at_query >= at_key), 0.0, -jnp.inf)
+
+    def attend(j, head):
+        low, high = key_range(j)
+        scores = lax.dot_general(
+            qkv[head, j * 256:high, :], qkv[QPK, low:high, :],
+            (((1,), (1,)), ((), ())), preferred_element_type=F32,
+        ) * HD ** (-0.5) + bias[j, :, 0:high - low]
+        weights = jnp.exp(scores - jnp.max(scores, axis=1, keepdims=True))
+        weights = (weights / jnp.sum(weights, axis=1, keepdims=True)).astype(BF16)
+        out_ref[j * 256:high, head * HD:(head + 1) * HD] = jnp.dot(
+            weights, qkv[QPK + 1, low:high, :], preferred_element_type=F32
+        ).astype(BF16)
+
     first, second, third = ORDER
-    for c in ORDER:
-        update(c)
-    own_pair(1)
-    inverse = lax.rsqrt(wait_all(msg_r, t, r_s, r_r, peers_a) / D + 1e-05)
-    for i in range(8):
-        inv[i * 128:(i + 1) * 128, :] = jnp.broadcast_to(inverse[i:i + 1, :], (128, 128)).T
-    for c in ORDER:
-        deal(c)
-    forward_pair(0)
+
+    def row_scales():
+        inverse = lax.rsqrt(wait_all(msg_r, t, r_s, r_r, peers_a) / D + 1e-05)
+        for i in range(8):
+            inv[i * 128:(i + 1) * 128, :] = jnp.broadcast_to(inverse[i:i + 1, :], (128, 128)).T
+
+    def prior_ready():
+        @pl.when(holds_prior)
+        def _():
+            prior_here.wait()
+
+        @pl.when(jnp.logical_not(holds_prior))
+        def _():
+            prior_push.wait_recv()
+
+    update(first)
 
     @pl.when(holds_prior)
     def _():
-        prior_here.wait()
-
-    @pl.when(jnp.logical_not(holds_prior))
-    def _():
-        prior_push.wait_recv()
-
+        prior_push.start()
+        prior_here.start()
+
+    update(second)
+    update(third)
+    r_pushes = send_all(msg_r, t, r_s, r_r, peers_a)
+    deal(first)
+    prior_ready()
     mix(first)
     along_z(first, 0)
+    deal(second)
+    deal(third)
+    own_pair(1)
+    row_scales()
     mix(second)
+    forward_pair(0)
     mix(third)
-    own_pair(2)
     across(first)
     along_z(first, 1)
     share(first, 0, quarter)
     along_z(second, 0)
+    own_pair(2)
     for j in range(4):
         normalize(y, j)
-    forward_pair(1)
+        mask(j)
     across(second)
     along_z(second, 1)
     share(second, 0, quarter)
     onward(first)
-    own_pair(3)
+    forward_pair(1)
     across(third)
+    share(third, 0, quarter)
     along_z(third, 0)
     along_z(third, 1)
-    share(third, 0, quarter)
     ready_pair(0)
     complete(first)
     multiply(0, first)
-    forward_pair(2)
+    own_pair(3)
     ready_pair(1)
     multiply(1, first)
     onward(second)
     finish(0, first)
-    finish(1, first)
+    forward_pair(2)
     complete(second)
     multiply(0, second)
     multiply(1, second)
-    forward_pair(3)
     onward(third)
+    finish(1, first)
     ready_pair(2)
     multiply(2, first)
     multiply(2, second)
     finish(0, second)
     finish(1, second)
+    attend(0, 1)
+    attend(0, 2)
+    forward_pair(3)
     complete(third)
     multiply(0, third)
     multiply(1, third)
     multiply(2, third)
+    attend(1, 1)
+    attend(1, 2)
     finish(2, first)
     finish(2, second)
     ready_pair(3)
     for c in ORDER:
         multiply(3, c)
+    attend(2, 1)
+    attend(2, 2)
     for j in range(3):
         finish(j, third)
-    for c in ORDER:
-        finish(3, c)
+        attend(j, 0)
+        attend(j, 3)
+    finish(3, first)
+    finish(3, second)
+    attend(3, 1)
+    attend(3, 2)
+    finish(3, third)
+    attend(3, 0)
+    attend(3, 3)
 
     for copy in tok_pushes + a_pushes + b_pushes + r_pushes:
         copy.wait_send()
@@ -410,17 +461,17 @@
         prior_push.wait_send()
 
 
-def project(master, moment, second, gradient, prior, tokens, gain, tables):
+def project(master, moment, second, gradient, prior, tokens, gain, tables, segments):
     dma = pltpu.SemaphoreType.DMA
     vmem = pl.BlockSpec(memory_space=pltpu.VMEM)
     hbm = pl.BlockSpec(memory_space=pl.ANY)
     return pl.pallas_call(
         project_kernel,
         out_shape=(
-            jax.ShapeDtypeStruct((QPK + 2, TOK, HD), BF16),
+            jax.ShapeDtypeStruct((TOK, QPK * HD), BF16),
             jax.ShapeDtypeStruct((8, 128), F32),
         ),
-        in_specs=[hbm] * 6 + [vmem] * 2,
+        in_specs=[hbm] * 6 + [vmem] * 3,
         out_specs=(vmem, vmem),
         scratch_shapes=[
             pltpu.VMEM((4, TOK, FEAT), BF16),
@@ -441,6 +492,8 @@
             pltpu.VMEM((3, 4, 256, 256), F32),
             pltpu.VMEM((3, 4, 256, 256), SUM_TYPE),
             pltpu.VMEM((3, 4, 256, 256), SUM_TYPE),
+            pltpu.VMEM((QPK + 2, TOK, HD), BF16),
+            pltpu.VMEM((4, 256, 768), F32),
             dma((6,)),
             dma((2, PIECES)), dma((2, PIECES)), dma((2, 4)), dma((2, 4)),
             dma((7,)), dma((7,)), dma((15,)), dma((15,)), dma((7,)), dma((7,)),
@@ -455,19 +508,17 @@
         cost_estimate=pl.CostEstimate(
             flops=2 * TOK * D * 768, bytes_accessed=24 * 1024 * 1024, transcendentals=0
         ),
-    )(master, moment, second, gradient, prior.reshape(8, 4, 256, 768), tokens, gain, tables)
+    )(master, moment, second, gradient, prior.reshape(8, 4, 256, 768), tokens, gain, tables, segments)
 
 
 BLOCK = 256
 
 
-def attend_kernel(
-    qkv_ref, clip_ref, seg_ref, master_ref, moment_ref, second_ref, grad_ref,
+def outputs_kernel(
+    clip_ref, master_ref, moment_ref, second_ref, grad_ref, attended_ref,
     new_master_ref, new_moment_ref, new_second_ref, out_ref,
 ):
-    place = pl.program_id(0)
-
-    def adam_rows(i, carry):
+    def step(i, carry):
         rows = pl.ds(pl.multiple_of(i * 32, 32), 32)
         clip = jnp.concatenate([clip_ref[0:1, :]] * 3, axis=1)
         new_master, new_moment, new_second = adam(
@@ -478,69 +529,35 @@
         new_second_ref[rows, :] = new_second
         return carry
 
-    lax.fori_loop(0, BLOCK // 32, adam_rows, 0)
-
-    for q in range(TOK // BLOCK):
-        @pl.when(place == q)
-        def _(q=q):
-            first = max(0, q - 2) * BLOCK
-            last = (q + 1) * BLOCK
-            width = last - first
-            segments = seg_ref[0:1, :].astype(F32)
-            column = jnp.concatenate(
-                [
-                    jnp.broadcast_to(segments[:, s:s + 128], (128, 128)).T
-                    for s in range(q * BLOCK, last, 128)
-                ],
-                axis=0,
-            )
-            same = jnp.concatenate([column] * (width // 128), axis=1) == segments[:, first:last]
-            at_query = lax.broadcasted_iota(jnp.int32, (BLOCK, width), 0) + q * BLOCK
-            at_key = lax.broadcasted_iota(jnp.int32, (BLOCK, width), 1) + first
-            allowed = same & (at_query >= at_key)
-            for head in range(QPK):
-                scores = lax.dot_general(
-                    qkv_ref[head, q * BLOCK:last, :], qkv_ref[QPK, first:last, :],
-                    (((1,), (1,)), ((), ())), preferred_element_type=F32,
-                ) * HD ** (-0.5)
-                scores = jnp.where(allowed, scores, -jnp.inf)
-                weights = jnp.exp(scores - jnp.max(scores, axis=1, keepdims=True))
-                weights = (weights / jnp.sum(weights, axis=1, keepdims=True)).astype(BF16)
-                out_ref[:, head * HD:(head + 1) * HD] = jnp.dot(
-                    weights, qkv_ref[QPK + 1, first:last, :], preferred_element_type=F32
-                ).astype(BF16)
-
-
-def attend(qkv, clip, segments, master, moment, second, gradient):
-    steps = TOK // BLOCK
+    lax.fori_loop(0, BLOCK // 32, step, 0)
+    out_ref[...] = attended_ref[...]
+
+
+def outputs(clip, master, moment, second, gradient, attended):
     rows = pl.BlockSpec((BLOCK, COLS), lambda i: (i, 0))
+    wide = pl.BlockSpec((BLOCK, QPK * HD), lambda i: (i, 0))
     return pl.pallas_call(
-        attend_kernel,
-        grid=(steps,),
+        outputs_kernel,
+        grid=(TOK // BLOCK,),
         out_shape=(
             jax.ShapeDtypeStruct((FEAT, COLS), F32),
             jax.ShapeDtypeStruct((FEAT, COLS), F32),
             jax.ShapeDtypeStruct((FEAT, COLS), F32),
             jax.ShapeDtypeStruct((TOK, QPK * HD), BF16),
         ),
-        in_specs=[
-            pl.BlockSpec((QPK + 2, TOK, HD), lambda i: (0, 0, 0)),
-            pl.BlockSpec((8, 128), lambda i: (0, 0)),
-            pl.BlockSpec((1, TOK), lambda i: (0, 0)),
-            rows, rows, rows, rows,
-        ],
-        out_specs=(rows, rows, rows, pl.BlockSpec((BLOCK, QPK * HD), lambda i: (i, 0))),
-        compiler_params=pltpu.CompilerParams(vmem_limit_bytes=48 * 1024 * 1024),
-    )(qkv, clip, segments, master, moment, second, gradient)
+        in_specs=[pl.BlockSpec((8, 128), lambda i: (0, 0)), rows, rows, rows, rows, wide],
+        out_specs=(rows, rows, rows, wide),
+        compiler_params=pltpu.CompilerParams(vmem_limit_bytes=32 * 1024 * 1024),
+    )(clip, master, moment, second, gradient, attended)
 
 
 def shards(master, moment, second, gradient, prior_weights, tokens, norm_gain, segment_ids):
-    qkv, clip = project(
+    attended, clip = project(
         master, moment, second, gradient, prior_weights, tokens[0], norm_gain.reshape(8, 1, FEAT),
-        jnp.asarray(rotary_tables()),
-    )
-    new_master, new_moment, new_second, attended = attend(
-        qkv, clip, segment_ids, master, moment, second, gradient
+        jnp.asarray(rotary_tables()), segment_ids,
+    )
+    new_master, new_moment, new_second, attended = outputs(
+        clip, master, moment, second, gradient, attended
     )
     return (new_master, new_moment, new_second, attended[None])
 

time: 144 us -> 127 us (0.88)
  Pallas kernels: 140 us -> 123 us
    pallas_call x2, Pallas kernels: 140 us -> 123 us  [the longest x1 119 us: project(): pl.pallas_call(project_kernel, out_shape=(jax.ShapeDtypeStruct((TOK, QPK...]
where the time goes in v3:
time: 127 us
  Pallas kernels  123 us (97%)
  local copies, waits for them, and re-layouts  3.31 us (3%)
    pallas_call x1, Pallas kernels, project(): pl.pallas_call(project_kernel, out_shape=(jax.ShapeDtypeStruct((TOK, QPK...  119 us
    pallas_call x1, Pallas kernels, outputs(): pl.pallas_call(outputs_kernel, grid=(TOK // BLOCK,), out_shape=(jax.Shape...  3.53 us
    unnamed x12, local copies, waits for them, and re-layouts  3.31 us

profile of v3, /device:TPU:1, one launch (start us, length us, event | category | flops | bytes accessed | tf_op | source)
XLA Modules:
  0.0 127.0 jit_solution(12183335428457966826)
XLA Ops:
  0.6 0.0 copy-start
  0.6 0.0 copy-start.1
  0.7 0.0 copy-start.4
  0.7 119.4 %shard_map.120 = (bf16[1024,512]{1,0:T(8,128)(2,1)}, f32[8,128]{1,0:T(8,128)}) custom-call(f32[1024,384]{1,0:T(8,128)} %master_ref.3, f32[1024,384]{1,0:T(8,128)} %moment_ref.3, f32[1024,384]{1,0:T(8,128)} %second_ref.3, bf16[1024,384]{1,0:T(8,128)(2,1)} %grad_ref.3, bf16[8,4,256,768]{3,2,1,0:T(8,128)(2,1)} %bitcast.4, bf16[1024,1024]{1,0:T(8,128)(2,1)} %bitcast.5, ...), custom_call_target="tpu_custom_call" | custom-call | flops 12884901888 | bytes 25165824 | tf_op jit(solution)/shard_map/pallas_call | solution.py:468
  120.1 0.0 copy-done
  120.1 0.0 copy-done.1
  120.1 0.0 copy-done.4
  120.1 0.0 copy-start.2
  120.2 1.4 %copy-done.2 = f32[1024,384]{1,0:T(8,128)S(1)} copy-done((f32[1024,384]{1,0:T(8,128)S(1)}, f32[1024,384]{1,0:T(8,128)}, u32[]{:S(2)}) %copy-start.2) | copy-done | bytes 1572888
  121.6 0.0 copy-start.3
  121.6 1.2 copy-done.3
  122.8 0.0 copy-start.5
  122.8 0.7 copy-done.5
  123.5 3.5 %shard_map.121 = (f32[1024,384]{1,0:T(8,128)}, f32[1024,384]{1,0:T(8,128)}, f32[1024,384]{1,0:T(8,128)}, bf16[1024,512]{1,0:T(8,128)(2,1)}) custom-call(f32[8,128]{1,0:T(8,128)S(1)} %copy-done.5, f32[1024,384]{1,0:T(8,128)S(1)} %copy-done, f32[1024,384]{1,0:T(8,128)S(1)} %copy-done.1, f32[1024,384]{1,0:T(8,128)S(1)} %copy-done.2, ...), custom_call_target="tpu_custom_call" | custom-call | tf_op jit(solution)/shard_map/pallas_call | solution.py:539
Async XLA Ops:
  0.6 119.5 %copy-start = (f32[1024,384]{1,0:T(8,128)S(1)}, f32[1024,384]{1,0:T(8,128)}, u32[]{:S(2)}) copy-start(f32[1024,384]{1,0:T(8,128)} %master_ref.3) | copy-start | bytes 4718596
  0.6 119.5 %copy-start.1 = (f32[1024,384]{1,0:T(8,128)S(1)}, f32[1024,384]{1,0:T(8,128)}, u32[]{:S(2)}) copy-start(f32[1024,384]{1,0:T(8,128)} %moment_ref.3) | copy-start | bytes 4718596
  0.7 119.5 %copy-start.4 = (bf16[1024,384]{1,0:T(8,128)(2,1)S(1)}, bf16[1024,384]{1,0:T(8,128)(2,1)}, u32[]{:S(2)}) copy-start(bf16[1024,384]{1,0:T(8,128)(2,1)} %grad_ref.3) | copy-start | bytes 2359300
  120.1 1.4 %copy-start.2 = (f32[1024,384]{1,0:T(8,128)S(1)}, f32[1024,384]{1,0:T(8,128)}, u32[]{:S(2)}) copy-start(f32[1024,384]{1,0:T(8,128)} %second_ref.3) | copy-start | bytes 4718596
  121.6 1.2 copy-start.3
  122.8 0.7 copy-start.5

commit v4 on v3

--- a/solution.py
+++ b/solution.py
@@ -28,8 +28,7 @@
 TOK = 1024
 FEAT = 1024
 COLS = 384
-PIECES = 8
-PIECE = TOK // PIECES
+GROUPS = ((0, 256), (256, 256), (512, 256), (768, 128), (896, 128))
 ORDER = (2, 1, 0)
 
 
@@ -141,7 +140,8 @@
     tok_pushes = []
 
     def tok_rows(piece):
-        return pl.ds(piece * PIECE, PIECE)
+        start, count = GROUPS[piece // 2]
+        return pl.ds(start + piece % 2 * (count // 2), count // 2)
 
     def own_pair(j):
         for piece in (2 * j, 2 * j + 1):
@@ -165,14 +165,15 @@
     def normalize(block, j):
         gain = gain_ref[l * 4 + block]
         cols = pl.ds(pl.multiple_of(block * FEAT, FEAT), FEAT)
+        start, count = GROUPS[j]
 
         def step(i, carry):
-            rows = pl.ds(pl.multiple_of(j * 256 + i * 32, 32), 32)
+            rows = pl.ds(pl.multiple_of(start + i * 32, 32), 32)
             scale = jnp.concatenate([inv[rows, :]] * (FEAT // 128), axis=1)
             normed[rows, cols] = (raw[block, rows, :].astype(F32) * scale * gain).astype(BF16)
             return carry
 
-        lax.fori_loop(0, 8, step, 0)
+        lax.fori_loop(0, count // 32, step, 0)
 
     def ready_pair(j):
         for way, source, where in ((0, y_down, at_y_up), (1, y_up, at_y_down)):
@@ -197,6 +198,12 @@
     msg_b[mine] = wait_all(msg_a, t, a_s, a_r, peers_a)
     b_pushes = send_all(msg_b, mine, b_s, b_r, peers_b)
     own_pair(0)
+
+    @pl.when(holds_prior)
+    def _():
+        prior_push.start()
+        prior_here.start()
+
     sums = wait_all(msg_b, mine, b_s, b_r, peers_b)
     overall = jnp.broadcast_to(jnp.sum(sums, keepdims=True), (8, 128))
     clip_ref[...] = jnp.minimum(1.0, clip_rms * math.sqrt(D * QKV) / (jnp.sqrt(overall) + 1e-06))
@@ -242,6 +249,11 @@
     def part_of(c, q, cols):
         return w.at[c, :, g, q, :, cols]
 
+    def cross(c, slot, q):
+        block = part_of(c, q, here)
+        hx_pushes[c, slot] = push(block, block, hx_s.at[c, slot], hx_r.at[c, slot], at_h)
+        hx_pushes[c, slot].start()
+
     def mix(c):
         for d in range(1, 4):
             block = y_in.at[c, (y + 4 - d) % 4]
@@ -250,9 +262,7 @@
             policy = y_in[c, block].astype(F32)
             prior = pri[block, :, c * 128:(c + 1) * 128].astype(F32)
             w[c, block, g, quarter, :, here] = (mix_share * policy + (1.0 - mix_share) * prior).astype(BF16)
-        block = part_of(c, quarter, here)
-        hx_pushes[c] = push(block, block, hx_s.at[c], hx_r.at[c], at_h)
-        hx_pushes[c].start()
+        cross(c, 0, quarter)
 
     def along_z(c, part):
         block = part_of(c, quarter, (here, there)[part])
@@ -265,9 +275,9 @@
         sib_pushes[c, slot] = push(block, block, sib_s.at[c, slot], sib_r.at[c, slot], at_core)
         sib_pushes[c, slot].start()
 
-    def across(c):
-        came = part_of(c, quarter, there)
-        push(came, came, hx_s.at[c], hx_r.at[c], at_h).wait_recv()
+    def across(c, slot, q):
+        came = part_of(c, q, there)
+        push(came, came, hx_s.at[c, slot], hx_r.at[c, slot], at_h).wait_recv()
 
     def onward(c):
         ways = ((0, quarter_down, at_z_up), (1, quarter_up, at_z_down))
@@ -281,35 +291,66 @@
         for way, q, where in ways:
             share(c, 1 + way, q)
 
+    quarters = (quarter, quarter_down, quarter_up, quarter_far)
+
+    def shared(c):
+        for slot, q in enumerate(quarters):
+            block = w.at[c, :, 1 - g, q]
+            push(block, block, sib_s.at[c, slot], sib_r.at[c, slot], at_core).wait_recv()
+
+    def half_of(c, q, way):
+        return w.at[c, :, g, q, pl.ds(way * 128, 128), here]
+
+    def onward_alone(c):
+        for way, q, where in ((0, quarter_down, at_z_up), (1, quarter_up, at_z_down)):
+            block = part_of(c, q, here)
+            push(block, block, zg_s.at[c, 0, way], zg_r.at[c, 0, way], where).wait_recv()
+            block = half_of(c, q, way)
+            zf_pushes[c, way] = push(block, block, zf_s.at[c, way], zf_r.at[c, way], where)
+            zf_pushes[c, way].start()
+            cross(c, 1 + way, q)
+
+    def far_alone(c):
+        for way, where in ((0, at_z_up), (1, at_z_down)):
+            block = half_of(c, quarter_far, way)
+            push(block, block, zf_s.at[c, way], zf_r.at[c, way], where).wait_recv()
+        cross(c, 3, quarter_far)
+
+    def complete_alone(c):
+        for slot, q in enumerate(quarters):
+            across(c, slot, q)
+            share(c, slot, q)
+        shared(c)
+
     def complete(c):
         for way, where in ((0, at_z_up), (1, at_z_down)):
             block = part_of(c, quarter_far, (here, there)[way])
             push(block, block, zf_s.at[c, way], zf_r.at[c, way], where).wait_recv()
         share(c, 3, quarter_far)
-        for slot, q in enumerate((quarter, quarter_down, quarter_up, quarter_far)):
-            block = w.at[c, :, 1 - g, q]
-            push(block, block, sib_s.at[c, slot], sib_r.at[c, slot], at_core).wait_recv()
+        shared(c)
 
     def multiply(j, c):
-        rows = pl.ds(j * 256, 256)
+        rows = pl.ds(*GROUPS[j])
 
         def half(panel):
             return jnp.dot(
                 normed[rows, :], w[c, :, panel].reshape(4 * FEAT, 256), preferred_element_type=F32
             )
 
-        ps_out[c, j] = half(1 - l).astype(SUM_TYPE)
-        ps_pushes[j, c] = push(ps_out.at[c, j], ps_in.at[c, j], ps_s.at[c, j], ps_r.at[c, j], at_x)
+        ps_out[c, rows, :] = half(1 - l).astype(SUM_TYPE)
+        ps_pushes[j, c] = push(
+            ps_out.at[c, rows, :], ps_in.at[c, rows, :], ps_s.at[c, j], ps_r.at[c, j], at_x
+        )
         ps_pushes[j, c].start()
-        own[c, j] = half(l)
+        own[c, rows, :] = half(l)
 
     def finish(j, c):
         ps_pushes[j, c].wait_recv()
+        start, count = GROUPS[j]
 
         def step(i, carry):
-            rows = pl.ds(pl.multiple_of(i * 64, 64), 64)
-            at = pl.ds(pl.multiple_of(j * 256 + i * 64, 64), 64)
-            pair = (own[c, j, rows, :] + ps_in[c, j, rows, :].astype(F32)) * D ** (-0.5)
+            at = pl.ds(pl.multiple_of(start + i * 64, 64), 64)
+            pair = (own[c, at, :] + ps_in[c, at, :].astype(F32)) * D ** (-0.5)
             for head, values in ((c, pair[:, 0:128]), (3 + c, pair[:, 128:256])):
                 if head < 5:
                     turned = jnp.concatenate([values[:, 64:], values[:, :64]], axis=1)
@@ -317,7 +358,7 @@
                 qkv[head, at, :] = values.astype(BF16)
             return carry
 
-        lax.fori_loop(0, 4, step, 0)
+        lax.fori_loop(0, count // 64, step, 0)
 
     def key_range(j):
         return max(0, j - 2) * 256, (j + 1) * 256
@@ -365,88 +406,86 @@
         def _():
             prior_push.wait_recv()
 
-    update(first)
-
-    @pl.when(holds_prior)
-    def _():
-        prior_push.start()
-        prior_here.start()
-
-    update(second)
-    update(third)
+    for c in ORDER:
+        update(c)
     r_pushes = send_all(msg_r, t, r_s, r_r, peers_a)
     deal(first)
+    deal(second)
     prior_ready()
     mix(first)
     along_z(first, 0)
-    deal(second)
     deal(third)
     own_pair(1)
-    row_scales()
     mix(second)
-    forward_pair(0)
-    mix(third)
-    across(first)
+    across(first, 0, quarter)
     along_z(first, 1)
     share(first, 0, quarter)
     along_z(second, 0)
+    mix(third)
+    forward_pair(0)
     own_pair(2)
-    for j in range(4):
+    row_scales()
+    for j in range(5):
         normalize(y, j)
-        mask(j)
-    across(second)
-    along_z(second, 1)
-    share(second, 0, quarter)
     onward(first)
-    forward_pair(1)
-    across(third)
+    across(third, 0, quarter)
     share(third, 0, quarter)
+    onward_alone(second)
     along_z(third, 0)
     along_z(third, 1)
+    forward_pair(1)
+    for j in range(4):
+        mask(j)
     ready_pair(0)
+    far_alone(second)
     complete(first)
     multiply(0, first)
+    forward_pair(2)
     own_pair(3)
+    own_pair(4)
     ready_pair(1)
     multiply(1, first)
-    onward(second)
-    finish(0, first)
-    forward_pair(2)
-    complete(second)
+    onward(third)
+    complete_alone(second)
     multiply(0, second)
     multiply(1, second)
-    onward(third)
-    finish(1, first)
     ready_pair(2)
     multiply(2, first)
     multiply(2, second)
+    forward_pair(3)
+    complete(third)
+    for j in range(3):
+        multiply(j, third)
+    forward_pair(4)
+    finish(0, first)
+    finish(1, first)
     finish(0, second)
-    finish(1, second)
     attend(0, 1)
     attend(0, 2)
-    forward_pair(3)
-    complete(third)
-    multiply(0, third)
-    multiply(1, third)
-    multiply(2, third)
+    finish(1, second)
     attend(1, 1)
     attend(1, 2)
-    finish(2, first)
-    finish(2, second)
     ready_pair(3)
     for c in ORDER:
         multiply(3, c)
+    finish(2, first)
+    finish(2, second)
     attend(2, 1)
     attend(2, 2)
+    ready_pair(4)
+    for c in ORDER:
+        multiply(4, c)
     for j in range(3):
         finish(j, third)
         attend(j, 0)
         attend(j, 3)
-    finish(3, first)
-    finish(3, second)
+    for c in ORDER:
+        finish(3, c)
+    finish(4, first)
+    finish(4, second)
     attend(3, 1)
     attend(3, 2)
-    finish(3, third)
+    finish(4, third)
     attend(3, 0)
     attend(3, 3)
 
@@ -489,21 +528,21 @@
             pltpu.VMEM((3, 4, 256, 128), BF16),
             pltpu.VMEM((3, 4, 256, 128), BF16),
             pltpu.VMEM((4, 256, COLS), BF16),
-            pltpu.VMEM((3, 4, 256, 256), F32),
-            pltpu.VMEM((3, 4, 256, 256), SUM_TYPE),
-            pltpu.VMEM((3, 4, 256, 256), SUM_TYPE),
+            pltpu.VMEM((3, TOK, 256), F32),
+            pltpu.VMEM((3, TOK, 256), SUM_TYPE),
+            pltpu.VMEM((3, TOK, 256), SUM_TYPE),
             pltpu.VMEM((QPK + 2, TOK, HD), BF16),
             pltpu.VMEM((4, 256, 768), F32),
             dma((6,)),
-            dma((2, PIECES)), dma((2, PIECES)), dma((2, 4)), dma((2, 4)),
+            dma((2, 10)), dma((2, 10)), dma((2, 5)), dma((2, 5)),
             dma((7,)), dma((7,)), dma((15,)), dma((15,)), dma((7,)), dma((7,)),
             dma, dma,
-            dma((3, 3)), dma((3, 3)), dma((3, 3)), dma((3, 3)), dma((3,)), dma((3,)),
+            dma((3, 3)), dma((3, 3)), dma((3, 3)), dma((3, 3)), dma((3, 4)), dma((3, 4)),
             dma((3, 2, 2)), dma((3, 2, 2)), dma((3, 2)), dma((3, 2)),
-            dma((3, 4)), dma((3, 4)), dma((3, 4)), dma((3, 4)),
+            dma((3, 4)), dma((3, 4)), dma((3, 5)), dma((3, 5)),
         ],
         compiler_params=pltpu.CompilerParams(
-            collective_id=0, has_side_effects=True, vmem_limit_bytes=60 * 1024 * 1024
+            collective_id=0, has_side_effects=True, vmem_limit_bytes=54 * 1024 * 1024
         ),
         cost_estimate=pl.CostEstimate(
             flops=2 * TOK * D * 768, bytes_accessed=24 * 1024 * 1024, transcendentals=0
@@ -547,7 +586,7 @@
         ),
         in_specs=[pl.BlockSpec((8, 128), lambda i: (0, 0)), rows, rows, rows, rows, wide],
         out_specs=(rows, rows, rows, wide),
-        compiler_params=pltpu.CompilerParams(vmem_limit_bytes=32 * 1024 * 1024),
+        compiler_params=pltpu.CompilerParams(vmem_limit_bytes=24 * 1024 * 1024),
     )(clip, master, moment, second, gradient, attended)
 
 

time: 127 us -> 121 us (0.953)
  Pallas kernels: 123 us -> 117 us
  local copies, waits for them, and re-layouts: 3.31 us -> 1.91 us
    pallas_call x1, Pallas kernels: 119 us -> 114 us  [project(): pl.pallas_call(project_kernel, out_shape=(jax.ShapeDtypeStruct((TOK, QPK...]
    unnamed x12, local copies, waits for them, and re-layouts: 3.31 us -> 1.91 us
where the time goes in v4:
time: 121 us; the launch traced here: 120 us
  Pallas kernels  117 us (97%)
  local copies, waits for them, and re-layouts  1.91 us (2%)
    pallas_call x1, Pallas kernels, project(): pl.pallas_call(project_kernel, out_shape=(jax.ShapeDtypeStruct((TOK, QPK...  114 us
    pallas_call x1, Pallas kernels, outputs(): pl.pallas_call(outputs_kernel, grid=(TOK // BLOCK,), out_shape=(jax.Shape...  3.53 us

profile of v4, /device:TPU:1, one launch (start us, length us, event | category | flops | bytes accessed | tf_op | source)
XLA Modules:
  0.0 120.0 jit_solution(16781297965984385007)
XLA Ops:
  0.6 0.0 copy-start
  0.6 0.0 copy-start.1
  0.7 0.0 copy-start.2
  0.7 0.0 copy-start.4
  0.7 113.8 %shard_map.120 = (bf16[1024,512]{1,0:T(8,128)(2,1)}, f32[8,128]{1,0:T(8,128)}) custom-call(f32[1024,384]{1,0:T(8,128)} %master_ref.3, f32[1024,384]{1,0:T(8,128)} %moment_ref.3, f32[1024,384]{1,0:T(8,128)} %second_ref.3, bf16[1024,384]{1,0:T(8,128)(2,1)} %grad_ref.3, bf16[8,4,256,768]{3,2,1,0:T(8,128)(2,1)} %bitcast.4, bf16[1024,1024]{1,0:T(8,128)(2,1)} %bitcast.5, ...), custom_call_target="tpu_custom_call" | custom-call | flops 12884901888 | bytes 25165824 | tf_op jit(solution)/shard_map/pallas_call | solution.py:507
  114.5 0.0 copy-done
  114.5 0.0 copy-done.1
  114.5 0.0 copy-done.2
  114.5 0.0 copy-done.4
  114.6 0.0 copy-start.3
  114.6 1.2 %copy-done.3 = bf16[1024,512]{1,0:T(8,128)(2,1)S(1)} copy-done((bf16[1024,512]{1,0:T(8,128)(2,1)S(1)}, bf16[1024,512]{1,0:T(8,128)(2,1)}, u32[]{:S(2)}) %copy-start.3) | copy-done | bytes 1048600
  115.8 0.0 copy-start.5
  115.8 0.7 copy-done.5
  116.5 3.5 %shard_map.121 = (f32[1024,384]{1,0:T(8,128)}, f32[1024,384]{1,0:T(8,128)}, f32[1024,384]{1,0:T(8,128)}, bf16[1024,512]{1,0:T(8,128)(2,1)}) custom-call(f32[8,128]{1,0:T(8,128)S(1)} %copy-done.5, f32[1024,384]{1,0:T(8,128)S(1)} %copy-done, f32[1024,384]{1,0:T(8,128)S(1)} %copy-done.1, f32[1024,384]{1,0:T(8,128)S(1)} %copy-done.2, ...), custom_call_target="tpu_custom_call" | custom-call | tf_op jit(solution)/shard_map/pallas_call | solution.py:578
Async XLA Ops:
  0.6 113.9 %copy-start = (f32[1024,384]{1,0:T(8,128)S(1)}, f32[1024,384]{1,0:T(8,128)}, u32[]{:S(2)}) copy-start(f32[1024,384]{1,0:T(8,128)} %master_ref.3) | copy-start | bytes 4718596
  0.6 113.9 %copy-start.1 = (f32[1024,384]{1,0:T(8,128)S(1)}, f32[1024,384]{1,0:T(8,128)}, u32[]{:S(2)}) copy-start(f32[1024,384]{1,0:T(8,128)} %moment_ref.3) | copy-start | bytes 4718596
  0.7 113.9 %copy-start.2 = (f32[1024,384]{1,0:T(8,128)S(1)}, f32[1024,384]{1,0:T(8,128)}, u32[]{:S(2)}) copy-start(f32[1024,384]{1,0:T(8,128)} %second_ref.3) | copy-start | bytes 4718596
  0.7 113.9 %copy-start.4 = (bf16[1024,384]{1,0:T(8,128)(2,1)S(1)}, bf16[1024,384]{1,0:T(8,128)(2,1)}, u32[]{:S(2)}) copy-start(bf16[1024,384]{1,0:T(8,128)(2,1)} %grad_ref.3) | copy-start | bytes 2359300
  114.6 1.2 %copy-start.3 = (bf16[1024,512]{1,0:T(8,128)(2,1)S(1)}, bf16[1024,512]{1,0:T(8,128)(2,1)}, u32[]{:S(2)}) copy-start(bf16[1024,512]{1,0:T(8,128)(2,1)} %get-tuple-element.11.attended_ref) | copy-start | bytes 3145732
  115.8 0.7 copy-start.5

commit v5 on v4

--- a/solution.py
+++ b/solution.py
@@ -61,9 +61,9 @@
 
 
 def project_kernel(
-    master_ref, moment_ref, second_ref, grad_ref, prior_ref, tok_ref, gain_ref, table_ref, seg_ref,
+    master_ref, moment_ref, second_ref, grad_ref, prior_ref, tok_ref, table_ref, gain_ref, seg_ref,
     out_ref, clip_ref,
-    raw, normed, w, mas, mom, sec, gra, inv, msg_a, msg_b, msg_r, z_out, z_in, y_in, pri, own, ps_out, ps_in, qkv, bias,
+    raw, normed, w, mas, mom, sec, gra, inv, msg_a, msg_b, msg_r, z_out, z_in, y_in, pri, own, ps_out, ps_in, qkv, bias, table,
     load_sem, tok_s, tok_r, fwd_s, fwd_r, a_s, a_r, b_s, b_r, r_s, r_r, pri_s, pri_r,
     za_s, za_r, ya_s, ya_r, hx_s, hx_r, zg_s, zg_r, zf_s, zf_r, sib_s, sib_r, ps_s, ps_r,
 ):
@@ -89,6 +89,7 @@
         pltpu.make_async_copy(master_ref, mas, load_sem.at[2]),
         pltpu.make_async_copy(moment_ref, mom, load_sem.at[3]),
         pltpu.make_async_copy(second_ref, sec, load_sem.at[4]),
+        pltpu.make_async_copy(table_ref, table, load_sem.at[6]),
     ]
     for load in loads:
         load.start()
@@ -354,7 +355,7 @@
             for head, values in ((c, pair[:, 0:128]), (3 + c, pair[:, 128:256])):
                 if head < 5:
                     turned = jnp.concatenate([values[:, 64:], values[:, :64]], axis=1)
-                    values = values * table_ref[0, at, :] + turned * table_ref[1, at, :]
+                    values = values * table[0, at, :] + turned * table[1, at, :]
                 qkv[head, at, :] = values.astype(BF16)
             return carry
 
@@ -510,7 +511,7 @@
             jax.ShapeDtypeStruct((TOK, QPK * HD), BF16),
             jax.ShapeDtypeStruct((8, 128), F32),
         ),
-        in_specs=[hbm] * 6 + [vmem] * 3,
+        in_specs=[hbm] * 7 + [vmem] * 2,
         out_specs=(vmem, vmem),
         scratch_shapes=[
             pltpu.VMEM((4, TOK, FEAT), BF16),
@@ -533,7 +534,8 @@
             pltpu.VMEM((3, TOK, 256), SUM_TYPE),
             pltpu.VMEM((QPK + 2, TOK, HD), BF16),
             pltpu.VMEM((4, 256, 768), F32),
-            dma((6,)),
+            pltpu.VMEM((2, TOK, HD), F32),
+            dma((7,)),
             dma((2, 10)), dma((2, 10)), dma((2, 5)), dma((2, 5)),
             dma((7,)), dma((7,)), dma((15,)), dma((15,)), dma((7,)), dma((7,)),
             dma, dma,
@@ -547,15 +549,15 @@
         cost_estimate=pl.CostEstimate(
             flops=2 * TOK * D * 768, bytes_accessed=24 * 1024 * 1024, transcendentals=0
         ),
-    )(master, moment, second, gradient, prior.reshape(8, 4, 256, 768), tokens, gain, tables, segments)
+    )(master, moment, second, gradient, prior.reshape(8, 4, 256, 768), tokens, tables, gain, segments)
 
 
 BLOCK = 256
 
 
 def outputs_kernel(
-    clip_ref, master_ref, moment_ref, second_ref, grad_ref, attended_ref,
-    new_master_ref, new_moment_ref, new_second_ref, out_ref,
+    clip_ref, master_ref, moment_ref, second_ref, grad_ref,
+    new_master_ref, new_moment_ref, new_second_ref,
 ):
     def step(i, carry):
         rows = pl.ds(pl.multiple_of(i * 32, 32), 32)
@@ -569,12 +571,10 @@
         return carry
 
     lax.fori_loop(0, BLOCK // 32, step, 0)
-    out_ref[...] = attended_ref[...]
-
-
-def outputs(clip, master, moment, second, gradient, attended):
+
+
+def outputs(clip, master, moment, second, gradient):
     rows = pl.BlockSpec((BLOCK, COLS), lambda i: (i, 0))
-    wide = pl.BlockSpec((BLOCK, QPK * HD), lambda i: (i, 0))
     return pl.pallas_call(
         outputs_kernel,
         grid=(TOK // BLOCK,),
@@ -582,12 +582,11 @@
             jax.ShapeDtypeStruct((FEAT, COLS), F32),
             jax.ShapeDtypeStruct((FEAT, COLS), F32),
             jax.ShapeDtypeStruct((FEAT, COLS), F32),
-            jax.ShapeDtypeStruct((TOK, QPK * HD), BF16),
         ),
-        in_specs=[pl.BlockSpec((8, 128), lambda i: (0, 0)), rows, rows, rows, rows, wide],
-        out_specs=(rows, rows, rows, wide),
+        in_specs=[pl.BlockSpec((8, 128), lambda i: (0, 0)), rows, rows, rows, rows],
+        out_specs=(rows, rows, rows),
         compiler_params=pltpu.CompilerParams(vmem_limit_bytes=24 * 1024 * 1024),
-    )(clip, master, moment, second, gradient, attended)
+    )(clip, master, moment, second, gradient)
 
 
 def shards(master, moment, second, gradient, prior_weights, tokens, norm_gain, segment_ids):
@@ -595,9 +594,7 @@
         master, moment, second, gradient, prior_weights, tokens[0], norm_gain.reshape(8, 1, FEAT),
         jnp.asarray(rotary_tables()), segment_ids,
     )
-    new_master, new_moment, new_second, attended = outputs(
-        clip, master, moment, second, gradient, attended
-    )
+    new_master, new_moment, new_second = outputs(clip, master, moment, second, gradient)
     return (new_master, new_moment, new_second, attended[None])
 
 

time: 121 us -> 120 us (level)
  no operation moved by 1% of the time
where the time goes in v5:
time: 120 us; the launch traced here: 119 us
  Pallas kernels  117 us (98%)
  local copies, waits for them, and re-layouts  1.66 us (1%)
    pallas_call x1, Pallas kernels, project(): pl.pallas_call(project_kernel, out_shape=(jax.ShapeDtypeStruct((TOK, QPK...  113 us
    pallas_call x1, Pallas kernels, outputs(): pl.pallas_call(outputs_kernel, grid=(TOK // BLOCK,), out_shape=(jax.Shape...  3.34 us

profile of v5, /device:TPU:1, one launch (start us, length us, event | category | flops | bytes accessed | tf_op | source)
XLA Modules:
  0.0 119.2 jit_solution(11349261257033789846)
XLA Ops:
  0.6 0.0 copy-start
  0.6 0.0 copy-start.1
  0.7 0.0 copy-start.2
  0.7 0.0 copy-start.3
  0.7 113.5 %shard_map.120 = (bf16[1024,512]{1,0:T(8,128)(2,1)}, f32[8,128]{1,0:T(8,128)}) custom-call(f32[1024,384]{1,0:T(8,128)} %master_ref.3, f32[1024,384]{1,0:T(8,128)} %moment_ref.3, f32[1024,384]{1,0:T(8,128)} %second_ref.3, bf16[1024,384]{1,0:T(8,128)(2,1)} %grad_ref.3, bf16[8,4,256,768]{3,2,1,0:T(8,128)(2,1)} %bitcast.5, bf16[1024,1024]{1,0:T(8,128)(2,1)} %bitcast.6, ...), custom_call_target="tpu_custom_call" | custom-call | flops 12884901888 | bytes 25165824 | tf_op jit(solution)/shard_map/pallas_call | solution.py:508
  114.1 0.0 copy-done
  114.1 0.0 copy-done.1
  114.2 0.0 copy-done.2
  114.2 0.0 copy-done.3
  114.2 0.0 copy-start.4
  114.2 0.7 copy-done.4
  114.9 0.0 copy-start.5
  114.9 3.3 %shard_map.121 = (f32[1024,384]{1,0:T(8,128)}, f32[1024,384]{1,0:T(8,128)}, f32[1024,384]{1,0:T(8,128)}) custom-call(f32[8,128]{1,0:T(8,128)S(1)} %copy-done.4, f32[1024,384]{1,0:T(8,128)S(1)} %copy-done, f32[1024,384]{1,0:T(8,128)S(1)} %copy-done.1, f32[1024,384]{1,0:T(8,128)S(1)} %copy-done.2, bf16[1024,384]{1,0:T(8,128)(2,1)S(1)} %copy-done.3), custom_call_target="tpu_custom_call" | custom-call | tf_op jit(solution)/shard_map/pallas_call | solution.py:578
  118.2 0.0 copy-done.5
  118.2 1.0 copy.14
Async XLA Ops:
  0.6 113.5 %copy-start = (f32[1024,384]{1,0:T(8,128)S(1)}, f32[1024,384]{1,0:T(8,128)}, u32[]{:S(2)}) copy-start(f32[1024,384]{1,0:T(8,128)} %master_ref.3) | copy-start | bytes 4718596
  0.6 113.5 %copy-start.1 = (f32[1024,384]{1,0:T(8,128)S(1)}, f32[1024,384]{1,0:T(8,128)}, u32[]{:S(2)}) copy-start(f32[1024,384]{1,0:T(8,128)} %moment_ref.3) | copy-start | bytes 4718596
  0.7 113.5 %copy-start.2 = (f32[1024,384]{1,0:T(8,128)S(1)}, f32[1024,384]{1,0:T(8,128)}, u32[]{:S(2)}) copy-start(f32[1024,384]{1,0:T(8,128)} %second_ref.3) | copy-start | bytes 4718596
  0.7 113.5 %copy-start.3 = (bf16[1024,384]{1,0:T(8,128)(2,1)S(1)}, bf16[1024,384]{1,0:T(8,128)(2,1)}, u32[]{:S(2)}) copy-start(bf16[1024,384]{1,0:T(8,128)(2,1)} %grad_ref.3) | copy-start | bytes 2359300
  114.2 0.7 copy-start.4
  114.9 3.3 %copy-start.5 = (bf16[1024,512]{1,0:T(8,128)(2,1)S(1)}, bf16[1024,512]{1,0:T(8,128)(2,1)}, u32[]{:S(2)}) copy-start(bf16[1024,512]{1,0:T(8,128)(2,1)} %get-tuple-element.13) | copy-start | bytes 3145732
